TPU v7x, 32 devices: a whole 2x2x4 slice. The times are simulated.
32 devices in a mesh: dp: 4 (over y, x), fsdp: 8 (over z, core).
Axes of the slice: x: 2, y: 2, z: 4, core: 2. Of those that a mesh axis runs over, the one named last changes fastest.
Arguments:
- layer_input: bfloat16 [32, 1024, 768], P(('dp', 'fsdp')), may hold values from -6 to 6
- lengths: int32 [32], P(('dp', 'fsdp')), may hold values from 64 to 1024, as said below
- ln1_gain: bfloat16 [768], P(('dp', 'fsdp')), may hold values from 0.099609375 to 1.8984375
- ln1_bias: bfloat16 [768], P(('dp', 'fsdp')), may hold values from -3 to 3
- w_qkv: bfloat16 [768, 2304], P(('dp', 'fsdp')), may hold values from -0.3125 to 0.3125
- b_qkv: bfloat16 [2304], P(('dp', 'fsdp')), may hold values from -3 to 3
- w_out: bfloat16 [768, 768], P(('dp', 'fsdp')), may hold values from -1.25 to 1.25
- b_out: bfloat16 [768], P(('dp', 'fsdp')), may hold values from -2 to 2
- ln2_gain: bfloat16 [768], P(('dp', 'fsdp')), may hold values from 0.099609375 to 1.8984375
- ln2_bias: bfloat16 [768], P(('dp', 'fsdp')), may hold values from -3 to 3
- w_up: bfloat16 [768, 3072], P(('dp', 'fsdp')), may hold values from -0.21875 to 0.21875
- b_up: bfloat16 [3072], P(('dp', 'fsdp')), may hold values from -3 to 3
- w_down: bfloat16 [3072, 768], P(('dp', 'fsdp')), may hold values from -0.109375 to 0.109375
- b_down: bfloat16 [768], P(('dp', 'fsdp')), may hold values from -2 to 2
- cotangent: bfloat16 [32, 1024, 768], P(('dp', 'fsdp')), may hold values from -6 to 6
Outputs:
- result: bfloat16 [32, 1024, 768], P(('dp', 'fsdp'))
- grad_input: float32 [32, 1024, 768], P(('dp', 'fsdp'))
- grad_ln1_gain: float32 [768], P(('dp', 'fsdp'))
- grad_ln1_bias: float32 [768], P(('dp', 'fsdp'))
- grad_w_qkv: float32 [768, 2304], P(('dp', 'fsdp'))
- grad_b_qkv: float32 [2304], P(('dp', 'fsdp'))
- grad_w_out: float32 [768, 768], P(('dp', 'fsdp'))
- grad_b_out: float32 [768], P(('dp', 'fsdp'))
- grad_ln2_gain: float32 [768], P(('dp', 'fsdp'))
- grad_ln2_bias: float32 [768], P(('dp', 'fsdp'))
- grad_w_up: float32 [768, 3072], P(('dp', 'fsdp'))
- grad_b_up: float32 [3072], P(('dp', 'fsdp'))
- grad_w_down: float32 [3072, 768], P(('dp', 'fsdp'))
- grad_b_down: float32 [768], P(('dp', 'fsdp'))
Inputs may be any that keep to these rules, and one draw needn't show every extreme that they name: `lengths`: some slot has length exactly 1024.
All inputs are finite; a program needn't handle non-finite values.
Results may differ from a plain program's by a relative error of at most 0.012.
The roundings to bfloat16 on the way count: a program that leaves them out, or rounds other values in their place, can miss the bound.
Values may be sent and summed in bfloat16 or wider, within the bound.
No kernel may reach another device: no remote copies, remote signals or barrier semaphores. Data moves between devices by JAX's collectives and lax.ppermute only.
A program may use at most 192 MiB of HBM per device.

v0:
```python
import functools
import itertools
import math

import jax
import jax.numpy as jnp
from jax import lax
from jax.experimental import pallas as pl
from jax.experimental.pallas import tpu as pltpu
from jax.sharding import PartitionSpec as P

H = 12
HD = 64
AXES = ("dp", "fsdp")
NORM_EPS = 1e-05
LOG2E = math.log2(math.e)
NT = (((1,), (1,)), ((), ()))
NN = (((1,), (0,)), ((), ()))
TN = (((0,), (0,)), ((), ()))
bf16 = jnp.bfloat16
f32 = jnp.float32
MIB = 2**20


def dot(a, b, dims):
    return lax.dot_general(a, b, dims, preferred_element_type=f32)


def whole(shape):
    return pl.BlockSpec(shape, lambda *i: (0,) * len(shape), pipeline_mode=pl.Buffered(1))


def smem():
    return pl.BlockSpec(memory_space=pltpu.SMEM)


def tie(value, *others):
    return lax.optimization_barrier((value, *others))[0]


def params(mib):
    return pltpu.CompilerParams(vmem_limit_bytes=mib * MIB)


def sds(shape, dtype):
    return jax.ShapeDtypeStruct(shape, dtype)


def cost(us):
    return pl.CostEstimate(flops=int(us * 1e9), bytes_accessed=0, transcendentals=0)


def norm_stats(values):
    mean = jnp.mean(values, axis=1, keepdims=True)
    centred = values - mean
    inverse = lax.rsqrt(jnp.mean(centred * centred, axis=1, keepdims=True) + NORM_EPS)
    return centred * inverse, inverse


def vector_layout(each, d, e, ff):
    return [(1, each * k, each) for k in range(6)] + [(0, 0, each * (e // d)), (0, 128, each * (ff // d))]


def prepare_kernel(idx_ref, *refs, layout, halves, nu):
    ins, (mine, theirs, mine_rest, theirs_rest) = refs[:12], refs[12:16]
    both, rest, low, down, sems = refs[16:21]
    small = refs[21:]
    wq, wo, wu, wd = ins[:4]
    each, e = wq.shape
    d = wo.shape[1]
    ff = wu.shape[1]
    targets = [both.at[:, :e], rest.at[:, :d], rest.at[:, d : d + ff], down]
    targets += list(small)
    copies = [pltpu.make_async_copy(ref, to, sems.at[k]) for k, (ref, to) in enumerate(zip(ins, targets))]
    for copy in copies:
        copy.start()
    low[...] = jnp.zeros_like(low)
    for copy in copies:
        copy.wait()
    for j in range(nu):
        rest[:, d + ff + j * d : d + ff + (j + 1) * d] = down[j * each : (j + 1) * each, :]
    for k, (row, lane, size) in enumerate(layout):
        low[row : row + 1, lane : lane + size] = small[k][...].astype(f32)
    both[:, e:] = low[...].astype(bf16)
    core = idx_ref[3]
    for ref, own, other, half in ((both, mine, theirs, halves[0]), (rest, mine_rest, theirs_rest, halves[1])):
        own[...] = ref[:, pl.ds(pl.multiple_of(core * half, 128), half)]
        other[...] = ref[:, pl.ds(pl.multiple_of((1 - core) * half, 128), half)]


def prepare(idx, wq, wo, wu, wd, vectors, layout):
    each, e = wq.shape
    d, ff = wo.shape[1], wu.shape[1]
    wide = d + 2 * ff
    halves = ((e + 256) // 2, wide // 2)
    return pl.pallas_call(
        functools.partial(prepare_kernel, layout=layout, halves=halves, nu=ff // d),
        in_specs=[smem()] + [pl.BlockSpec(memory_space=pltpu.HBM)] * 12,
        out_shape=[sds((each, h), bf16) for h in halves for _ in range(2)],
        scratch_shapes=[
            pltpu.VMEM((each, e + 256), bf16),
            pltpu.VMEM((each, wide), bf16),
            pltpu.VMEM((each, 256), f32),
            pltpu.VMEM(wd.shape, bf16),
            pltpu.SemaphoreType.DMA((12,)),
        ]
        + [pltpu.VMEM((1, v.shape[0]), bf16) for v in vectors],
        compiler_params=params(60),
    )(idx, wq, wo, wu, wd, *[v.reshape(1, -1) for v in vectors])


def gathered_chip(idx_ref, k, at):
    x, y, z = (idx_ref[i] for i in range(3))
    first, deep = at // 4, z ^ ((at // 2) % 2 + 2 * (at % 2))
    second = k % 2
    if (k // 2) % 2 == 0:
        return ((y ^ second) * 2 + (x ^ first)) * 4 + deep
    return ((y ^ first) * 2 + (x ^ second)) * 4 + deep


def qkv_kernel(idx_ref, x_ref, *rest, n, each, layout, pieces):
    parts, (a_ref, o_ref, w_ref), vecs, low = rest[:pieces], rest[pieces : pieces + 3], rest[pieces + 3 : -1], rest[-1]
    quarter = w_ref.shape[3]
    e = o_ref.shape[1]

    @pl.when(pl.program_id(0) == 0)
    def _():
        if pieces == 1:
            for k in range(4):
                w_ref[k] = parts[0][:, k * quarter : (k + 1) * quarter].reshape(w_ref.shape[1:])
        else:
            core = idx_ref[3]
            for k, part in enumerate(parts):
                quarter_at = 2 * (core if k < 4 else 1 - core) + (k // 2) % 2
                for at in range(8):
                    w_ref[quarter_at, gathered_chip(idx_ref, k, at)] = part[at]
        low[...] = w_ref[3, :, :, quarter - 256 :].astype(f32)
        for dev in range(n):
            for out, (row, lane, size) in zip(vecs, layout):
                at = dev * each + row
                out[:, dev * size : (dev + 1) * size] = low[at // 48, at % 48 : at % 48 + 1, lane : lane + size]

    normal, _ = norm_stats(x_ref[...].astype(f32))
    a = (normal * vecs[0][...] + vecs[1][...]).astype(bf16)
    a_ref[...] = a
    for k in range(4):
        cols = slice(k * quarter, min((k + 1) * quarter, e))
        wide = cols.stop - cols.start
        w = w_ref[k].reshape(a.shape[1], quarter)
        o_ref[:, cols] = (dot(a, w[:, :wide], NN) + vecs[6][:, cols]).astype(bf16)


def qkv_call(idx, x, parts, n, layout, e, rb=256):
    s, d = x.shape
    each = d // n
    quarter = (e + 256) // 4
    sizes = [n * size for _, _, size in layout]
    return pl.pallas_call(
        functools.partial(qkv_kernel, n=n, each=each, layout=layout, pieces=len(parts)),
        grid=(s // rb,),
        in_specs=[smem(), pl.BlockSpec((rb, d), lambda i: (i, 0))] + [whole(p.shape) for p in parts],
        out_specs=[
            pl.BlockSpec((rb, d), lambda i: (i, 0)),
            pl.BlockSpec((rb, e), lambda i: (i, 0)),
            whole((4, d // 48, 48, quarter)),
        ]
        + [whole((1, size)) for size in sizes],
        out_shape=[sds((s, d), bf16), sds((s, e), bf16), sds((4, d // 48, 48, quarter), bf16)]
        + [sds((1, size), f32) for size in sizes],
        scratch_shapes=[pltpu.VMEM((d // 48, 48, 256), f32)],
        compiler_params=params(60),
        cost_estimate=cost(9),
    )(idx, x, *parts)


def fwd_kernel(len_ref, q_ref, k_ref, v_ref, *refs, qb, nq, rc):
    s_ref, z_ref, m_ref = refs[-3:]
    o_ref, rz_ref, *kept = refs[-5 - 2 * nq : -3]
    p_refs, a_refs = kept[:nq], kept[nq:]
    n = len_ref[0]
    lane = lax.broadcasted_iota(jnp.int32, (1, 128), 1)

    def emit(blocks):
        units = [(i, h) for i in blocks for h in range(2)]

        def scores(t):
            i, h = units[t]
            q = q_ref[i * qb : (i + 1) * qb, :] * jnp.asarray(HD**-0.5, bf16)
            mine = (lane < HD) if h == 0 else (lane >= HD)
            nk = (i + 1) * qb
            s_ref[t % 2, :, :nk] = dot(jnp.where(mine, q, jnp.zeros_like(q)), k_ref[:nk, :], NT)

        def weights(t):
            i, h = units[t]
            for r0 in range(0, qb, rc):
                rr = slice(r0, r0 + rc)
                row = lax.broadcasted_iota(jnp.int32, (rc, qb), 0) + r0
                col = lax.broadcasted_iota(jnp.int32, (rc, qb), 1)
                mask = (col <= row) & (col < n - i * qb)
                top = jnp.where(mask, jnp.abs(s_ref[t % 2, rr, i * qb : (i + 1) * qb]), 0.0)
                for j in range(i):
                    top = jnp.maximum(top, jnp.abs(s_ref[t % 2, rr, j * qb : (j + 1) * qb]))
                top = jnp.max(top, axis=1, keepdims=True)
                top = jnp.sqrt(top * top + 1.0)
                total = jnp.zeros((rc, qb), f32)
                for j in range(i + 1):
                    cols = slice(j * qb, (j + 1) * qb)
                    s = s_ref[t % 2, rr, cols]
                    square = s * s + 1.0
                    inv = lax.rsqrt(square)
                    e = jnp.exp(square * inv - top)
                    if j == i:
                        e = jnp.where(mask, e, 0.0)
                    total = total + e
                    p_refs[i][h, rr, cols] = (s * inv * e).astype(bf16)
                    a_refs[i][h, rr, cols] = ((1.0 - inv * inv * (1.0 - inv)) * e).astype(bf16)
                rz = 1.0 / jnp.sum(total, axis=1, keepdims=True)
                z_ref[t % 2, rr, :] = jnp.broadcast_to(rz, (rc, 128))

        def mix(t):
            i, h = units[t]
            rows = slice(i * qb, (i + 1) * qb)
            rz = z_ref[t % 2]
            mixed = dot(p_refs[i][h], v_ref[: (i + 1) * qb, :], NN) * rz
            if h == 0:
                m_ref[...] = mixed
                rz_ref[rows, :] = rz
            else:
                o_ref[rows, :] = jnp.where(lane < HD, m_ref[...], mixed).astype(bf16)
                rz_ref[rows, :] = jnp.where(lane < HD, rz_ref[rows, :], rz)

        scores(0)
        for t in range(len(units)):
            if t + 1 < len(units):
                scores(t + 1)
            weights(t)
            mix(t)

    by_blocks(n, qb, nq, emit, lambda rows: dead_block(rows, (o_ref, rz_ref)))


def dead_block(rows, refs):
    for ref in refs:
        ref[rows, :] = jnp.zeros((rows.stop - rows.start, ref.shape[1]), ref.dtype)


def by_blocks(n, qb, nq, emit, dead):
    @pl.when(n > (nq - 1) * qb)
    def _():
        emit(list(range(nq)))

    @pl.when(n <= (nq - 1) * qb)
    def _():
        for i in range(nq):

            @pl.when(n > i * qb)
            def _():
                emit([i])

            @pl.when(n <= i * qb)
            def _():
                dead(slice(i * qb, (i + 1) * qb))


def attention_forward(lens, qkv, first, groups, before=(), deps=(), qb=256):
    s = qkv.shape[0]
    nq = s // qb
    hp = H // 2

    def columns(off):
        return pl.BlockSpec((s, 128), lambda g: (0, first + g + off))

    kept_shape = [sds((H, qb, (i + 1) * qb), bf16) for i in range(nq)]
    kept_spec = [pl.BlockSpec((2, qb, (i + 1) * qb), lambda g: (first + g, 0, 0)) for i in range(nq)]
    return pl.pallas_call(
        functools.partial(fwd_kernel, qb=qb, nq=nq, rc=32),
        grid=(groups,),
        in_specs=[smem(), columns(0), columns(hp), columns(2 * hp)] + [pl.BlockSpec(memory_space=pl.ANY)] * len(before),
        out_specs=[columns(0)] * 2 + kept_spec * 2,
        out_shape=[sds((s, H * HD), bf16), sds((s, H * HD), f32)] + kept_shape * 2,
        input_output_aliases={4 + k: k for k in range(len(before))},
        scratch_shapes=[
            pltpu.VMEM((2, qb, s), f32),
            pltpu.VMEM((2, qb, 128), f32),
            pltpu.VMEM((qb, 128), f32),
        ],
        compiler_params=params(60),
        cost_estimate=cost(7.5 * groups),
    )(tie(lens, *deps), qkv, qkv, qkv, *before)


def bwd_kernel(len_ref, q_ref, k_ref, v_ref, o_ref, rz_ref, d_ref, *rest, qb, nq, rc):
    p_refs, a_refs = rest[:nq], rest[nq : 2 * nq]
    out, dk_ref, dv_ref, dp_ref, ds_ref, low_ref, total_ref, low_t, q_t, dq_ref = rest[-10:]
    n = len_ref[0]
    scale = HD ** (-0.5)
    lane = lax.broadcasted_iota(jnp.int32, (1, 128), 1)
    dk_ref[...] = jnp.zeros_like(dk_ref)
    dv_ref[...] = jnp.zeros_like(dv_ref)

    def emit(blocks):
        units = [(i, h) for i in blocks for h in range(2)]

        def weight_grads(t):
            i, h = units[t]
            nk = (i + 1) * qb
            mine = (lane < HD) if h == 0 else (lane >= HD)
            if h == 0:
                rows = slice(i * qb, (i + 1) * qb)
                grad = d_ref[rows, :] * rz_ref[rows, :]
                low = grad.astype(bf16)
                along = grad * o_ref[rows, :].astype(f32)
                low_ref[i % 2] = low
                low_t[i % 2] = low.T
                q_t[i % 2] = q_ref[rows, :].T
                for k in range(2):
                    half = jnp.where((lane < HD) if k == 0 else (lane >= HD), along, 0.0)
                    total_ref[i % 2, k] = jnp.broadcast_to(jnp.sum(half, axis=1, keepdims=True), (qb, 128))
            low = low_ref[i % 2]
            dp_ref[t % 2, :, :nk] = dot(jnp.where(mine, low, jnp.zeros_like(low)), v_ref[:nk, :], NT)

        def score_grads(t):
            i, h = units[t]
            for r0 in range(0, qb, rc):
                rr = slice(r0, r0 + rc)
                total = jnp.concatenate([total_ref[i % 2, h, rr, :]] * (qb // 128), axis=1)
                for j in range(i + 1):
                    cols = slice(j * qb, (j + 1) * qb)
                    first = a_refs[i][h, rr, cols].astype(f32) * dp_ref[t % 2, rr, cols]
                    ds_ref[t % 2, rr, cols] = (first - p_refs[i][h, rr, cols].astype(f32) * total).astype(bf16)

        def grads(t):
            i, h = units[t]
            nk = (i + 1) * qb
            part = slice(h * HD, (h + 1) * HD)
            ds = ds_ref[t % 2, :, :nk]
            dq = dot(ds, k_ref[:nk, :], NN)
            if h == 0:
                dq_ref[...] = dq
            else:
                out[0, i * qb : nk, :] = (jnp.where(lane < HD, dq_ref[...], dq) * scale).astype(bf16)
            dv_ref[part, :nk] += dot(low_t[i % 2, part, :], p_refs[i][h], NN)
            dk_ref[part, :nk] += dot(q_t[i % 2, part, :], ds, NN)

        weight_grads(0)
        for t in range(len(units)):
            if t + 1 < len(units):
                weight_grads(t + 1)
            score_grads(t)
            grads(t)

    by_blocks(n, qb, nq, emit, lambda rows: dead_block(rows, (out.at[0],)))
    out[1] = (dk_ref[...] * scale).T.astype(bf16)
    out[2] = dv_ref[...].T.astype(bf16)


def attention_backward(lens, qkv, o, rz, dol, kept, deps=(), qb=256, first=0, groups=H // 2):
    s = qkv.shape[0]
    nq = s // qb
    hp = H // 2

    def columns(off):
        return pl.BlockSpec((s, 128), lambda g: (0, first + g + off))

    kept_spec = [pl.BlockSpec((2, qb, (i + 1) * qb), lambda g: (first + g, 0, 0)) for i in range(nq)]
    return pl.pallas_call(
        functools.partial(bwd_kernel, qb=qb, nq=nq, rc=64),
        grid=(groups,),
        in_specs=[smem(), columns(0), columns(hp), columns(2 * hp)] + [columns(0)] * 3 + kept_spec * 2,
        out_specs=pl.BlockSpec((3, s, 128), lambda g: (0, 0, g)),
        out_shape=sds((3, s, 128 * groups), bf16),
        scratch_shapes=[pltpu.VMEM((128, s), f32)] * 2
        + [
            pltpu.VMEM((2, qb, s), f32),
            pltpu.VMEM((2, qb, s), bf16),
            pltpu.VMEM((2, qb, 128), bf16),
            pltpu.VMEM((2, 2, qb, 128), f32),
            pltpu.VMEM((2, 128, qb), bf16),
            pltpu.VMEM((2, 128, qb), bf16),
            pltpu.VMEM((qb, 128), f32),
        ],
        compiler_params=params(60),
        cost_estimate=cost(26),
    )(tie(lens, *deps), qkv, qkv, qkv, o, rz, dol, *kept)


def ffn_kernel(len_ref, idx_ref, x_ref, o_ref, ct_ref, *rest, rb, n, nu, pieces, cut):
    parts, rest = rest[:pieces], rest[pieces:]
    bo_ref, g2_ref, b2_ref, bu_ref, bd_ref = rest[:5]
    (y_ref, g_ref, du_ref, c_ref, dyl_ref, drl_ref, dr_ref, dol_ref) = rest[5:13]
    sbd, sbu, sg2, sb2, sbo, w_ref, wd, sems = rest[13:]
    i = pl.program_id(0)
    d = x_ref.shape[1]
    each = d // n
    chips, rows, wide = w_ref.shape

    def weight(at):
        return w_ref[:, :, at : at + d].reshape(d, d)

    @pl.when(i == 0)
    def _():
        if pieces == 1:
            copies = [pltpu.make_async_copy(parts[0], w_ref, sems.at[0])]
        else:
            copies = []
            half = wide // 2
            core = idx_ref[3]
            for k, part in enumerate(parts):
                who, later = core if k < 4 else 1 - core, (k // 2) % 2
                lane = pl.multiple_of(who * half + later * cut, 128)
                for at in range(8):
                    to = w_ref.at[gathered_chip(idx_ref, k, at), :, pl.ds(lane, half - cut if later else cut)]
                    copies.append(pltpu.make_async_copy(part.at[at], to, sems.at[k * 8 + at]))
        for copy in copies:
            copy.start()
        for s in (sbd, sbu, sg2, sb2, sbo):
            s[...] = jnp.zeros_like(s)
        for copy in copies:
            copy.wait()
        for dev in range(n):
            for j in range(nu):
                at = (dev * nu + j) * each
                row = dev * each
                lane = (1 + nu + j) * d
                wd[at : at + each, :] = w_ref[row // rows, row % rows : row % rows + each, lane : lane + d]

    live = (lax.broadcasted_iota(jnp.int32, (rb, 1), 0) + i * rb) < len_ref[0]
    r = x_ref[...].astype(f32) + dot(o_ref[...], weight(0), NN) + bo_ref[...]
    n2, k2 = norm_stats(r)
    g2 = g2_ref[...]
    c = (n2 * g2 + b2_ref[...]).astype(bf16)
    c_ref[...] = c
    dyl = jnp.where(live, ct_ref[...], jnp.zeros((), bf16))
    dyl_ref[...] = dyl
    y = r + bd_ref[...]
    dc = jnp.zeros_like(r)
    k0 = math.sqrt(2 / math.pi)
    for j in range(nu):
        cols = slice(j * d, (j + 1) * d)
        wu = weight((1 + j) * d)
        wdj = wd[cols, :]
        u = dot(c, wu, NN) + bu_ref[:, cols]
        t = dot(dyl, wdj, NT)
        u2 = u * u
        hp = 0.5 + 0.5 * jnp.tanh(u * (k0 + (k0 * 0.044715) * u2))
        g = (u * hp).astype(bf16)
        slope = hp + u * (2.0 * hp * (1.0 - hp)) * (k0 + (3 * k0 * 0.044715) * u2)
        du = (t * slope).astype(bf16)
        g_ref[:, cols] = g
        du_ref[:, cols] = du
        y = y + dot(g, wdj, NN)
        dc = dc + dot(du, wu, NT)
        sbu[:, cols] += jnp.sum(du.astype(f32), axis=0, keepdims=True)
    y_ref[...] = jnp.where(live, y, 0.0).astype(bf16)
    q2 = dc * g2
    inner = q2 - jnp.mean(q2, axis=1, keepdims=True) - n2 * jnp.mean(q2 * n2, axis=1, keepdims=True)
    dr = dyl.astype(f32) + k2 * inner
    dr_ref[...] = dr
    drl = dr.astype(bf16)
    drl_ref[...] = drl
    dol_ref[...] = dot(drl, weight(0), NT)
    sbd[...] += jnp.sum(dyl.astype(f32), axis=0, keepdims=True)
    sg2[...] += jnp.sum(dc * n2, axis=0, keepdims=True)
    sb2[...] += jnp.sum(dc, axis=0, keepdims=True)
    sbo[...] += jnp.sum(drl.astype(f32), axis=0, keepdims=True)


def ffn_call(lens, idx, x, o, ct, parts, bo, g2, b2, bu, bd, n, cut, rb=256):
    s, d = x.shape
    ff = bu.shape[1]
    nu = ff // d
    wide = d + 2 * ff

    def row(w):
        return pl.BlockSpec((rb, w), lambda i: (i, 0))

    def acc(w):
        return pl.BlockSpec((1, w), lambda i: (0, 0))

    return pl.pallas_call(
        functools.partial(ffn_kernel, rb=rb, n=n, nu=nu, pieces=len(parts), cut=cut),
        grid=(s // rb,),
        in_specs=[smem(), smem(), row(d), row(d), row(d)]
        + [pl.BlockSpec(memory_space=pltpu.HBM)] * len(parts)
        + [whole((1, d)), whole((1, d)), whole((1, d)), whole((1, ff)), whole((1, d))],
        out_specs=[row(d), row(ff), row(ff), row(d), row(d), row(d), row(d), row(d)]
        + [acc(d), acc(ff), acc(d), acc(d), acc(d)],
        out_shape=[
            sds((s, d), bf16),
            sds((s, ff), bf16),
            sds((s, ff), bf16),
            sds((s, d), bf16),
            sds((s, d), bf16),
            sds((s, d), bf16),
            sds((s, d), f32),
            sds((s, d), f32),
            sds((1, d), f32),
            sds((1, ff), f32),
            sds((1, d), f32),
            sds((1, d), f32),
            sds((1, d), f32),
        ],
        scratch_shapes=[
            pltpu.VMEM((d // 48, 48, wide), bf16),
            pltpu.VMEM((ff, d), bf16),
            pltpu.SemaphoreType.DMA((64,)),
        ],
        compiler_params=params(60),
        cost_estimate=cost(37),
    )(lens, idx, x, o, ct, *parts, bo, g2, b2, bu, bd)


def wgrad_kernel(a_ref, b_ref, o_ref):
    b = b_ref[0] if len(b_ref.shape) == 3 else b_ref[...]
    o_ref[...] = dot(a_ref[...], b, TN).astype(o_ref.dtype)


def wgrad(a, b, ta, tb):
    s, m = a.shape
    if b.ndim == 3:
        n = b.shape[0] * b.shape[2]
        b_spec = pl.BlockSpec((1, s, b.shape[2]), lambda i, j: (j, 0, 0))
        tb = b.shape[2]
    else:
        n = b.shape[1]
        b_spec = pl.BlockSpec((s, tb), lambda i, j: (0, j))
    return pl.pallas_call(
        wgrad_kernel,
        grid=(m // ta, n // tb),
        in_specs=[pl.BlockSpec((s, ta), lambda i, j: (0, i)), b_spec],
        out_specs=pl.BlockSpec((ta, tb), lambda i, j: (i, j)),
        out_shape=sds((m, n), bf16),
        compiler_params=params(40),
        cost_estimate=cost(9),
    )(a, b)


def by_core(idx_ref, grad, keep, send, each):
    pairs = grad.reshape(grad.shape[0] // (2 * each), 2, each, grad.shape[1])
    first = idx_ref[3] == 0
    keep[...] = jnp.where(first, pairs[:, 0], pairs[:, 1]).astype(bf16)
    send[...] = jnp.where(first, pairs[:, 1], pairs[:, 0]).astype(bf16)


def down_kernel(idx_ref, g_ref, b_ref, keep, send, *, each, nu):
    grad = dot(g_ref[...], b_ref[...], TN)
    d = grad.shape[1]
    chips = grad.shape[0] // (2 * each * nu)
    parts = grad.reshape(chips, 2, nu, each, d)
    first = idx_ref[3] == 0
    for j in range(nu):
        cols = slice(j * d, (j + 1) * d)
        keep[:, :, cols] = jnp.where(first, parts[:, 0, j], parts[:, 1, j]).astype(bf16)
        send[:, :, cols] = jnp.where(first, parts[:, 1, j], parts[:, 0, j]).astype(bf16)


def down_grad(idx, g, dyl, n):
    s, ff = g.shape
    d = dyl.shape[1]
    each, nu = d // n, ff // d
    chips = n // 2 // nu
    spec = pl.BlockSpec((chips, each, ff), lambda i: (i, 0, 0))
    return pl.pallas_call(
        functools.partial(down_kernel, each=each, nu=nu),
        grid=(nu,),
        in_specs=[smem(), pl.BlockSpec((s, d), lambda i: (0, i)), whole((s, d))],
        out_specs=[spec, spec],
        out_shape=[sds((n // 2, each, ff), bf16)] * 2,
        compiler_params=params(60),
        cost_estimate=cost(9),
    )(idx, g, dyl)


def up_kernel(idx_ref, c_ref, du_ref, keep, send, *, each):
    by_core(idx_ref, dot(c_ref[...], du_ref[...], TN), keep, send, each)


def up_grad(idx, c, du, n):
    s, d = c.shape
    ff = du.shape[1]
    each = d // n
    spec = pl.BlockSpec((n // 2, each, d), lambda j: (0, 0, j))
    return pl.pallas_call(
        functools.partial(up_kernel, each=each),
        grid=(ff // d,),
        in_specs=[smem(), whole((s, d)), pl.BlockSpec((s, d), lambda j: (0, j))],
        out_specs=[spec, spec],
        out_shape=[sds((n // 2, each, ff), bf16)] * 2,
        compiler_params=params(60),
        cost_estimate=cost(9),
    )(idx, c, du)


def attention_grads_kernel(idx_ref, a_ref, dqkv_ref, o_ref, drl_ref, *rest, each):
    keep_a, send_a, keep_b, send_b = rest[-4:]
    j = pl.program_id(0)

    @pl.when(j < 2)
    def _():
        by_core(idx_ref, dot(a_ref[...], dqkv_ref[0], TN), keep_a, send_a, each)

    @pl.when(j == 2)
    def _():
        by_core(idx_ref, dot(a_ref[...], dqkv_ref[0], TN), keep_b, send_b, each)

    @pl.when(j == 3)
    def _():
        by_core(idx_ref, dot(o_ref[...], drl_ref[...], TN), keep_b, send_b, each)


def attention_grads(idx, a, dqkv, o, drl, n, deps=()):
    s, d = a.shape
    each = d // n
    spec_a = pl.BlockSpec((n // 2, each, d), lambda j: (0, 0, jnp.minimum(j, 1)))
    spec_b = pl.BlockSpec((n // 2, each, d), lambda j: (0, 0, jnp.maximum(j - 2, 0)))
    return pl.pallas_call(
        functools.partial(attention_grads_kernel, each=each),
        grid=(4,),
        in_specs=[
            smem(),
            whole((s, d)),
            pl.BlockSpec((1, s, d), lambda j: (jnp.minimum(j, 2), 0, 0)),
            whole((s, d)),
            whole((s, d)),
        ]
       ,
        out_specs=[spec_a, spec_a, spec_b, spec_b],
        out_shape=[sds((n // 2, each, 2 * d), bf16)] * 4,
        compiler_params=params(60),
        cost_estimate=cost(40),
    )(tie(idx, *deps), a, dqkv, o, drl)


def first_kernel(x_ref, dr_ref, dq_ref, w_ref, g_ref, sbo, sg2, sb2, sbd, sbu, *rest):
    gi_ref, out = rest[-2:]
    i = pl.program_id(0)
    d = x_ref.shape[1]
    quarter = w_ref.shape[3]

    @pl.when(i == 0)
    def _():
        out[:, : 5 * d] = jnp.zeros((1, 5 * d), f32)
        for k, ref in enumerate((sbo, sg2, sb2, sbd)):
            out[:, (5 + k) * d : (6 + k) * d] = ref[...]
        out[:, 9 * d :] = sbu[...]

    normal, inverse = norm_stats(x_ref[...].astype(f32))
    da = jnp.zeros(normal.shape, f32)
    for k in range(4):
        w = w_ref[k].reshape(d, quarter)
        at = k * quarter
        while at < min((k + 1) * quarter, 3 * d):
            j = at // d
            end = min((k + 1) * quarter, (j + 1) * d)
            part = dq_ref[j, :, at - j * d : end - j * d]
            da = da + dot(part, w[:, at - k * quarter : end - k * quarter], NT)
            out[:, 2 * d + at : 2 * d + end] += jnp.sum(part.astype(f32), axis=0, keepdims=True)
            at = end
    q1 = da * g_ref[...]
    inner = (
        q1 - jnp.mean(q1, axis=1, keepdims=True) - normal * jnp.mean(q1 * normal, axis=1, keepdims=True)
    )
    gi_ref[...] = dr_ref[...] + inverse * inner
    out[:, :d] += jnp.sum(da * normal, axis=0, keepdims=True)
    out[:, d : 2 * d] += jnp.sum(da, axis=0, keepdims=True)


def first_backward(x, dr, dqkv, w, gain, sums, deps=(), rb=256):
    s, d = x.shape

    def row(w):
        return pl.BlockSpec((rb, w), lambda i: (i, 0))

    wide = 9 * d + sums[-1].shape[1]
    return pl.pallas_call(
        first_kernel,
        grid=(s // rb,),
        in_specs=[row(d), row(d), pl.BlockSpec((3, rb, d), lambda i: (0, i, 0)), whole(w.shape), whole((1, d))]
        + [whole(t.shape) for t in sums]
       ,
        out_specs=[row(d), pl.BlockSpec((1, wide), lambda i: (0, 0))],
        out_shape=[sds((s, d), f32), sds((1, wide), f32)],
        compiler_params=params(60),
        cost_estimate=cost(10),
    )(x, dr, dqkv, w, tie(gain, *deps), *sums)


def scatter_sum(buf, n, order):
    lin = lax.axis_index(AXES)
    bits = n.bit_length() - 1
    rest = buf.shape[1:]
    buf = buf.reshape((2,) * bits + rest)
    left = list(range(bits - 1, -1, -1))
    for step, b in enumerate(order):
        axis = left.index(b)
        left.pop(axis)
        bit = (lin >> b) & 1
        send = lax.dynamic_index_in_dim(buf, 1 - bit, axis, keepdims=False)
        keep = lax.dynamic_index_in_dim(buf, bit, axis, keepdims=False)
        got = lax.ppermute(send, AXES, [(i, i ^ (1 << b)) for i in range(n)])
        buf = keep.astype(f32) + got.astype(f32)
        if step < bits - 1:
            buf = buf.astype(send.dtype)
    return buf


def permute(x, mask, n=32):
    return lax.ppermute(x, AXES, [(i, i ^ mask) for i in range(n)])


CORE, XBIT, YBIT = 1, 8, 16


def join(block, got):
    return jnp.concatenate([block[None], got[None]])


def gather_cores(mine, theirs, core):
    got = permute(theirs, CORE)
    return jnp.where(core == 0, jnp.concatenate([mine, got]), jnp.concatenate([got, mine]))


def gather_first(block, cut):
    a, b = block[..., :cut], block[..., cut:]
    return a, permute(a, XBIT), b, permute(b, YBIT)


def gather_second(a, b):
    parts = (a, permute(a, YBIT), b, permute(b, XBIT))
    return [t.reshape((8,) + t.shape[-2:]) for t in parts]


def fold_kernel(idx_ref, *refs, plan, joined):
    ins, outs = refs[: 2 * len(plan)], refs[-2 if joined else -2 * len(plan) :]
    lane = 0
    for k, (dim, which) in enumerate(plan):
        kept, got = ins[2 * k], ins[2 * k + 1]
        lead, wide = kept.shape[:-2], kept.shape[-1]
        for side in range(2):
            out = outs[side if joined else 2 * k + side]
            at = idx_ref[which] if side == 0 else 1 - idx_ref[which]
            for t in itertools.product(*[range(m) for m in lead[:dim] + lead[dim + 1 :]]):
                source = t[:dim] + (at,) + t[dim:]
                value = (kept[source].astype(f32) + got[source].astype(f32)).astype(bf16)
                if joined:
                    out[t + (slice(None), slice(lane, lane + wide))] = value
                else:
                    out[t] = value
        lane += wide


def fold(idx, pairs, plan, us, deps=(), joined=False):
    stepped = pairs[0][0].ndim > 3 and not joined
    args, in_specs, out_specs, out_shape, total = [], [], [], [], 0
    for (kept, got), (dim, _) in zip(pairs, plan):
        lead, (each, wide) = kept.shape[:-2], kept.shape[-2:]
        left = lead[:dim] + lead[dim + 1 :]
        total += wide
        args += [kept, got]

        def spec(shape):
            if not stepped:
                return pl.BlockSpec()
            m = len(shape)
            return pl.BlockSpec(shape[:-3] + (1,) + shape[-2:], lambda i: (0,) * (m - 3) + (i, 0, 0))

        in_specs += [spec(kept.shape)] * 2
        out_specs += [spec(left + (each, wide))] * 2
        out_shape += [sds(left + (each, wide), bf16)] * 2
    if joined:
        out_specs, out_shape = [pl.BlockSpec()] * 2, [sds(left + (each, total), bf16)] * 2
    grid = {"grid": (pairs[0][0].shape[-3],)} if stepped else {}
    return pl.pallas_call(
        functools.partial(fold_kernel, plan=plan, joined=joined),
        in_specs=[smem()] + in_specs,
        out_specs=out_specs,
        out_shape=out_shape,
        compiler_params=params(24),
        cost_estimate=cost(us),
        **grid,
    )(tie(idx, *deps), *args)


def last_kernel(kept, got, *refs, cuts):
    outs = refs[-len(cuts) :]
    total = kept[...].astype(f32) + got[...].astype(f32)
    each = total.shape[0]
    at = 0
    for out, (rows, wide) in zip(outs, cuts):
        for j in range(rows):
            out[j * each : (j + 1) * each, :] = total[:, at : at + wide]
            at += wide


def fold_last(kept, got, cuts, deps=()):
    each = kept.shape[0]
    return pl.pallas_call(
        functools.partial(last_kernel, cuts=cuts),
        in_specs=[pl.BlockSpec()] * 2,
        out_specs=[pl.BlockSpec()] * len(cuts),
        out_shape=[sds((rows * each, wide), f32) for rows, wide in cuts],
        compiler_params=params(24),
        cost_estimate=cost(1),
    )(tie(kept, *deps), got)


def body(
    n,
    dp,
    layer_input,
    lengths,
    ln1_gain,
    ln1_bias,
    w_qkv,
    b_qkv,
    w_out,
    b_out,
    ln2_gain,
    ln2_bias,
    w_up,
    b_up,
    w_down,
    b_down,
    cotangent,
):
    s, d = layer_input.shape[1:]
    x = layer_input.reshape(s, d)
    ct = cotangent.reshape(s, d)
    e, ff = w_qkv.shape[1], w_up.shape[1]
    each = d // n
    nu = ff // d
    fast = n == 32 and dp == 4
    lin = lax.axis_index(AXES)
    idx = jnp.stack([(lin >> 3) & 1, (lin >> 4) & 1, (lin >> 1) & 3, lin & 1, (lin >> 1) & 1, (lin >> 2) & 1]).astype(jnp.int32)
    vectors = (ln1_gain, ln1_bias, b_out, ln2_gain, ln2_bias, b_down, b_qkv, b_up)
    layout = vector_layout(each, d, e, ff)
    mine, theirs, mine_rest, theirs_rest = prepare(idx, w_qkv, w_out, w_up, w_down, vectors, layout)
    cut_q, cut_r = (e + 256) // 4, 128 * (-(-(d + 2 * ff) // 512))
    if fast:
        core = lin & 1
        q = gather_cores(mine, theirs, core)
        r = gather_cores(mine_rest, theirs_rest, core)
        q = join(q, permute(q, 4))
        q = tie(q, r)
        q = join(q, permute(q, 2))
        r = tie(r, q)
        a0, a1, b0, b1 = gather_first(q, cut_q)
        got_r = permute(r, 4)
        qa, qb = join(a0, a1), join(b0, b1)
        parts = gather_second(qa, qb)
        r = join(r, tie(got_r, qa, qb))
        parts[1], parts[3] = tie(parts[1], r), tie(parts[3], r)
        parts += [permute(t, CORE) for t in parts]
        ra, rb = r[..., :cut_r], r[..., cut_r:]
        ra, rb = join(ra, permute(ra, 2)), join(rb, permute(rb, 2))
        got_ra, got_rb = permute(ra, XBIT), permute(rb, YBIT)
        x_in = tie(x, ra, rb)
    else:
        def gathered(own, other):
            both = jnp.where((lin & 1) == 0, jnp.concatenate([own, other], 1), jnp.concatenate([other, own], 1))
            return lax.all_gather(both, AXES, axis=0, tiled=True)

        x_in = x
        parts = [gathered(mine, theirs)]
        rest = [gathered(mine_rest, theirs_rest).reshape(d // 48, 48, d + 2 * ff)]
    a, qkv, wq, g1, b1, bo, g2, b2, bd, bq, bu = qkv_call(idx, x_in, parts, n, layout, e)
    if fast:
        ra, rb = join(ra, tie(got_ra, qkv)), join(rb, tie(got_rb, qkv))
        ra, ga, rb, gb = gather_second(ra, rb)
        o, rz, *kept = attention_forward(lengths, qkv, 0, H // 2, deps=(ra, rb))
        other_ra, other_rb = permute(ra, CORE), permute(rb, CORE)
        ga, gb = tie(ga, o, other_ra, other_rb), tie(gb, o, other_ra, other_rb)
        rest = [ra, ga, rb, gb, other_ra, permute(ga, CORE), other_rb, permute(gb, CORE)]
    else:
        o, rz, *kept = attention_forward(lengths, qkv, 0, H // 2)
    (y, g, du, c, dyl, drl, dr, dol, sbd, sbu, sg2, sb2, sbo) = ffn_call(
        lengths, idx, x, o, ct, rest, bo, g2, b2, bu, bd, n, cut_r
    )
    sums = (sbo, sg2, sb2, sbd, sbu)
    if fast:
        core_x, core_y, deep_0, deep_1 = 0, 1, 4, 5

        def chips(t):
            return t.reshape((2, 2, 4) + t.shape[1:])

        def deep(t):
            return t.reshape((2, 2) + t.shape[1:])

        keep_d, send_d = down_grad(idx, g, dyl, n)
        got_d = permute(send_d, CORE)
        keep_u, send_u = up_grad(idx, c, du, n)
        got_u = permute(send_u, CORE)
        kd, sd = fold(idx, [(chips(keep_d), chips(got_d))], [(1, core_x)], 2.5, deps=(keep_u,))
        rd = permute(sd, XBIT)
        ku, su = fold(idx, [(chips(keep_u), chips(got_u))], [(0, core_y)], 2.5, deps=(kd,))
        ru = permute(su, YBIT)
        dqkv = attention_backward(lengths, qkv, o, rz, dol, kept, deps=(ku,))
        kd, sd, ku, su = fold(idx, [(kd, rd), (ku, ru)], [(0, core_y), (0, core_x)], 2.5, deps=(dqkv,))
        rd, ru = permute(sd, YBIT), permute(su, XBIT)
        ka, sa, kb, sb = attention_grads(idx, a, dqkv, o, drl, n, deps=(kd,))
        ga, gb = permute(sa, CORE), permute(sb, CORE)
        pairs = [(deep(kd), deep(rd)), (deep(ku), deep(ru))]
        kw, sw = fold(idx, pairs, [(1, deep_0)] * 2, 30, deps=(ka,), joined=True)
        rw = permute(sw, 2)
        pairs = [(chips(ka), chips(ga)), (chips(kb), chips(gb))]
        ka, sa, kb, sb = fold(idx, pairs, [(1, core_x), (0, core_y)], 2.5, deps=(kw,))
        ra, rb = permute(sa, XBIT), permute(sb, YBIT)
        grad_input, total = first_backward(x, dr, dqkv, wq, g1, sums, deps=(ka,))
        got = permute(total, CORE)
        kw, sw = fold(idx, [(kw, rw)], [(0, deep_1)], 1, deps=(total,))
        rw = permute(sw, 4)
        ka, sa, kb, sb = fold(idx, [(ka, ra), (kb, rb)], [(0, core_y), (0, core_x)], 1, deps=(kw,))
        ra, rb = permute(sa, YBIT), permute(sb, XBIT)
        total = total + tie(got, ka)
        got = [permute(total, mask) for mask in (XBIT, YBIT, XBIT | YBIT)]
        grad_down, grad_up = fold_last(kw, rw, [(nu, d), (1, ff)], deps=(ra, rb))
        got = lax.optimization_barrier((*got, grad_up))
        total = total + got[0] + got[1] + got[2]
        pairs = [(deep(ka), deep(ra)), (deep(kb), deep(rb))]
        kq, sq = fold(idx, pairs, [(1, deep_0)] * 2, 1, deps=(grad_up, total), joined=True)
        rq = permute(sq, 2)
        got = [permute(total, mask) for mask in (2, 4, 6)]
        kq, sq = fold(idx, [(kq, rq)], [(0, deep_1)], 1)
        rq = permute(sq, 4)
        got = lax.optimization_barrier((*got, kq))
        total = total + got[0] + got[1] + got[2]
        grad_qkv, grad_out = fold_last(kq, rq, [(1, e), (1, d)])
    else:
        order = list(range(n.bit_length() - 1))
        grad_down = scatter_sum(wgrad(g, dyl, d, d).reshape(n, ff // n, d), n, order)
        grad_up = scatter_sum(wgrad(c, du, d, d).reshape(n, each, ff), n, order)
        grad_out = scatter_sum(wgrad(o, drl, d, d).reshape(n, each, d), n, order)
        dqkv = attention_backward(lengths, qkv, o, rz, dol, kept)
        grad_qkv = scatter_sum(wgrad(a, dqkv, d, d).reshape(n, each, e), n, order)
        grad_input, total = first_backward(x, dr, dqkv, wq, g1, sums)
        total = lax.psum(total, AXES)
    shares, at = [], 0
    for size in (each, each, 3 * each, each, each, each, each, nu * each):
        shares.append(lax.dynamic_slice_in_dim(total[0], at + lin * size, size))
        at += n * size
    gs1, gb1, gbq, gbo, gs2, gb2, gbd, gbu = shares
    return (
        y.reshape(layer_input.shape),
        grad_input.reshape(layer_input.shape),
        gs1,
        gb1,
        grad_qkv,
        gbq,
        grad_out,
        gbo,
        gs2,
        gb2,
        grad_up,
        gbu,
        grad_down,
        gbd,
    )


def solution(mesh):
    split = P(AXES)
    wide = P(AXES, None)
    cube = P(AXES, None, None)
    in_specs = (
        cube, split, split, split, wide, split, wide, split, split, split, wide, split, wide, split, cube,
    )
    out_specs = (
        cube, cube, split, split, wide, split, wide, split, split, split, wide, split, wide, split,
    )
    n = mesh.shape["dp"] * mesh.shape["fsdp"]
    return jax.shard_map(
        functools.partial(body, n, mesh.shape["dp"]),
        mesh=mesh,
        in_specs=in_specs,
        out_specs=out_specs,
        check_vma=False,
    )
```

profile of v0, /device:TPU:0, one launch (start us, length us, event | category | flops | bytes accessed | tf_op | source)
XLA Modules:
  0.0 293.0 jit_solution(5869996814264223634)
XLA Ops:
  1.3 2.6 shard_map.254
  6.5 4.0 %collective-permute-start.2 = (bf16[48,1280]{1,0:T(8,128)(2,1)S(1)}, bf16[48,1280]{1,0:T(8,128)(2,1)S(1)}, u32[]{:S(2)}, u32[]{:S(2)}) collective-permute-start(bf16[48,1280]{1,0:T(8,128)(2,1)S(1)} %maximum_select_fusion.2), channel_id=1, source_target_pairs={{0,4},{1,5},{2,6},{3,7},{4,0},{5,1},{6,2},{7,3},{8,12},{9,13},{10,... | collective-permute-start | bytes 368648 | tf_op jit(solution)/shard_map/ppermute | solution.py:708
  12.5 4.3 %collective-permute-done.2 = bf16[48,1280]{1,0:T(8,128)(2,1)S(1)} collective-permute-done((bf16[48,1280]{1,0:T(8,128)(2,1)S(1)}, bf16[48,1280]{1,0:T(8,128)(2,1)S(1)}, u32[]{:S(2)}, u32[]{:S(2)}) %collective-permute-start.2) | collective-permute-done | bytes 122912 | tf_op jit(solution)/shard_map/ppermute | solution.py:708
  17.6 6.8 %collective-permute-done.3 = bf16[2,48,1280]{2,1,0:T(8,128)(2,1)S(1)} collective-permute-done((bf16[2,48,1280]{2,1,0:T(8,128)(2,1)S(1)}, bf16[2,48,1280]{2,1,0:T(8,128)(2,1)S(1)}, u32[]{:S(2)}, u32[]{:S(2)}) %collective-permute-start.3) | collective-permute-done | bytes 245792 | tf_op jit(solution)/shard_map/ppermute | solution.py:708
  24.4 1.3 collective-permute-start.6
  25.7 1.5 collective-permute-start.5
  27.2 3.0 %collective-permute-start.4 = (bf16[48,3456]{1,0:T(8,128)(2,1)S(1)}, bf16[48,3456]{1,0:T(8,128)(2,1)S(1)}, u32[]{:S(2)}, u32[]{:S(2)}) collective-permute-start(bf16[48,3456]{1,0:T(8,128)(2,1)S(1)} %maximum_select_fusion), channel_id=1, source_target_pairs={{0,4},{1,5},{2,6},{3,7},{4,0},{5,1},{6,2},{7,3},{8,12},{9,13},{10,... | collective-permute-start | bytes 995336 | tf_op jit(solution)/shard_map/ppermute | solution.py:708
  32.2 1.6 collective-permute-start.10
  33.8 10.5 %collective-permute-done.4 = bf16[48,3456]{1,0:T(8,128)(2,1)S(1)} collective-permute-done((bf16[48,3456]{1,0:T(8,128)(2,1)S(1)}, bf16[48,3456]{1,0:T(8,128)(2,1)S(1)}, u32[]{:S(2)}, u32[]{:S(2)}) %collective-permute-start.4) | collective-permute-done | bytes 331808 | tf_op jit(solution)/shard_map/ppermute | solution.py:708
  45.1 1.4 collective-permute-start.7
  47.2 7.6 %collective-permute-done.9 = bf16[2,48,1664]{2,1,0:T(8,128)(2,1)S(1)} collective-permute-done((bf16[2,48,1664]{2,1,0:T(8,128)(2,1)S(1)}, bf16[2,48,1664]{2,1,0:T(8,128)(2,1)S(1)}, u32[]{:S(2)}, u32[]{:S(2)}) %collective-permute-start.9) | collective-permute-done | bytes 319520 | tf_op jit(solution)/shard_map/ppermute | solution.py:708
  55.0 5.3 %collective-permute-done.7 = bf16[2,48,1792]{2,1,0:T(8,128)(2,1)S(1)} collective-permute-done((bf16[2,48,1792]{2,1,0:T(8,128)(2,1)S(1)}, bf16[2,48,1792]{2,1,0:T(8,128)(2,1)S(1)}, u32[]{:S(2)}, u32[]{:S(2)}) %collective-permute-start.7) | collective-permute-done | bytes 344096 | tf_op jit(solution)/shard_map/ppermute | solution.py:708
  63.1 10.3 %shard_map.255 = (bf16[1024,768]{1,0:T(8,128)(2,1)}, bf16[1024,2304]{1,0:T(8,128)(2,1)}, bf16[4,16,48,640]{3,2,1,0:T(8,128)(2,1)}, f32[1,768]{1,0:T(1,128)}, f32...) custom-call(s32[6]{0:T(128)} %stack.27.idx_ref, ...), custom_call_target="tpu_custom_call" | custom-call | flops 8999999488 | tf_op jit(solution)/shard_map/pallas_call | solution.py:158
  73.4 1.5 collective-permute-done.16
  76.8 2.3 collective-permute-start.17
  79.1 25.2 %shard_map.256 = (bf16[1024,768]{1,0:T(8,128)(2,1)}, f32[1024,768]{1,0:T(8,128)}, bf16[12,256,256]{2,1,0:T(8,128)(2,1)}, bf16[12,256,512]{2,1,0:T(8,128)(2,1)}, ...) custom-call(s32[1]{0:T(128)S(6)} %copy.29.len_ref, ...), custom_call_target="tpu_custom_call" | custom-call | flops 44999999488 | tf_op jit(solution)/shard_map/pallas_call | solution.py:275
  104.4 5.2 %collective-permute-done.17 = bf16[2,2,2,48,1792]{4,3,2,1,0:T(8,128)(2,1)} collective-permute-done((bf16[2,2,2,48,1792]{4,3,2,1,0:T(8,128)(2,1)S(1)}, bf16[2,2,2,48,1792]{4,3,2,1,0:T(8,128)(2,1)}, u32[]{:S(2)}, u32[]{:S(2)}) %collective-permute-start.17) | collective-permute-done | bytes 1376288 | tf_op jit(solution)/shard_map/ppermute | solution.py:708
  110.1 4.7 %collective-permute-done.22.rest_7_ = bf16[8,48,1664]{2,1,0:T(8,128)(2,1)S(1)} collective-permute-done((bf16[8,48,1664]{2,1,0:T(8,128)(2,1)}, bf16[8,48,1664]{2,1,0:T(8,128)(2,1)S(1)}, u32[]{:S(2)}, u32[]{:S(2)}) %collective-permute-start.22) | collective-permute-done | bytes 1277984 | tf_op jit(solution)/shard_map/ppermute | solution.py:708
  116.2 37.3 %shard_map.257 = (bf16[1024,768]{1,0:T(8,128)(2,1)}, bf16[1024,3072]{1,0:T(8,128)(2,1)}, bf16[1024,3072]{1,0:T(8,128)(2,1)}, bf16[1024,768]{1,0:T(8,128)(2,1)}, ...) custom-call(s32[1]{0:T(128)S(6)} %copy.29.len_ref, ...), custom_call_target="tpu_custom_call" | custom-call | flops 36999999488 | tf_op jit(solution)/shard_map/pallas_call | solution.py:480
  153.6 9.3 %shard_map.259 = (bf16[16,24,3072]{2,1,0:T(8,128)(2,1)}, bf16[16,24,3072]{2,1,0:T(8,128)(2,1)}) custom-call(s32[6]{0:T(128)} %stack.27.idx_ref, bf16[1024,3072]{1,0:T(8,128)(2,1)} %get-tuple-element.146.g_ref, bf16[1024,768]{1,0:T(8,128)(2,1)} %get-tuple-element.147.b_ref), custom_call_target="tpu_custom_call" | custom-call | flops 8999999488 | tf_op jit(solution)/shard_map/pallas_call | solution.py:563
  163.0 9.4 %shard_map.258 = (bf16[16,24,3072]{2,1,0:T(8,128)(2,1)}, bf16[16,24,3072]{2,1,0:T(8,128)(2,1)}) custom-call(s32[6]{0:T(128)} %stack.27.idx_ref, bf16[1024,768]{1,0:T(8,128)(2,1)} %get-tuple-element.142.c_ref, bf16[1024,3072]{1,0:T(8,128)(2,1)} %get-tuple-element.143.du_ref), custom_call_target="tpu_custom_call" | custom-call | flops 8999999488 | tf_op jit(solution)/shard_map/pallas_call | solution.py:583
  172.8 1.7 copy-done.2
  174.5 1.6 shard_map.260
  177.2 2.7 shard_map.261
  180.9 2.6 collective-permute-start.26
  183.4 21.1 %shard_map.262.dqkv_ref.dq_ref = bf16[3,1024,768]{2,1,0:T(8,128)(2,1)} custom-call(s32[1]{0:T(128)S(6)} %copy.29.len_ref, bf16[1024,2304]{1,0:T(8,128)(2,1)} %get-tuple-element.128.q_ref.k_ref.v_ref, bf16[1024,2304]{1,0:T(8,128)(2,1)} %get-tuple-element.128.q_ref.k_ref.v_ref, bf16[1024,2304]{1,0:T(8,128)(2,1)} %get-tuple-element.128.q_ref.k_ref.v_ref, ...), custom_call_target="tpu_custom_call" | custom-call | flops 25999998976 | tf_op jit(solution)/shard_map/pallas_call | solution.py:366
  204.6 5.6 %collective-permute-done.26.refs_3_ = bf16[2,4,24,3072]{3,2,1,0:T(8,128)(2,1)S(1)} collective-permute-done((bf16[2,4,24,3072]{3,2,1,0:T(8,128)(2,1)}, bf16[2,4,24,3072]{3,2,1,0:T(8,128)(2,1)S(1)}, u32[]{:S(2)}, u32[]{:S(2)}) %collective-permute-start.26) | collective-permute-done | bytes 1179680 | tf_op jit(solution)/shard_map/ppermute | solution.py:708
  210.1 1.3 collective-permute-done.25.refs_1_
  211.4 1.3 copy-done.17
  212.7 1.3 copy-done.19
  213.9 1.5 shard_map.263
  218.0 10.7 %shard_map.264 = (bf16[16,24,1536]{2,1,0:T(8,128)(2,1)}, bf16[16,24,1536]{2,1,0:T(8,128)(2,1)}, bf16[16,24,1536]{2,1,0:T(8,128)(2,1)}, bf16[16,24,1536]{2,1,0:T(8,128)(2,1)}) custom-call(s32[6]{0:T(128)} %stack.27.idx_ref, bf16[1024,768]{1,0:T(8,128)(2,1)} %get-tuple-element.172.a_ref, bf16[3,1024,768]{2,1,0:T(8,128)(2,1)} %shard_map.262.dqkv_ref.dq_ref, ...), custom_call_target="tpu_custom_call" | custom-call | flops 40000000000 | tf_op jit(solution)/shard_map/pallas_call | solution.py:616
  229.2 2.4 collective-permute-done.27
  234.8 2.0 collective-permute-start.32
  236.8 1.6 shard_map.266
  241.9 10.8 %shard_map.267 = (f32[1024,768]{1,0:T(8,128)}, f32[1,9984]{1,0:T(1,128)}) custom-call(bf16[1024,768]{1,0:T(8,128)(2,1)} %bitcast.136, f32[1024,768]{1,0:T(8,128)} %get-tuple-element.141.dr_ref, bf16[3,1024,768]{2,1,0:T(8,128)(2,1)} %shard_map.262.dqkv_ref.dq_ref, bf16[4,16,48,640]{3,2,1,0:T(8,128)(2,1)} %get-tuple-element.165.w_ref, ...), custom_call_target="tpu_custom_call" | custom-call | flops 10000000000 | tf_op jit(solution)/shard_map/pallas_call | solution.py:675
  256.7 1.4 collective-permute-start.39
  258.1 3.4 %collective-permute-start.40 = (bf16[24,6144]{1,0:T(8,128)(2,1)S(1)}, bf16[24,6144]{1,0:T(8,128)(2,1)S(1)}, u32[]{:S(2)}, u32[]{:S(2)}) collective-permute-start(bf16[24,6144]{1,0:T(8,128)(2,1)S(1)} %get-tuple-element.205), channel_id=1, source_target_pairs={{0,4},{1,5},{2,6},{3,7},{4,0},{5,1},{6,2},{7,3},{8,12},{9,13},{10,... | collective-permute-start | bytes 884744 | tf_op jit(solution)/shard_map/ppermute | solution.py:708
  261.5 1.2 collective-permute-done.31
  262.8 1.8 collective-permute-start.35
  264.6 1.2 collective-permute-start.36
  266.3 5.8 %collective-permute-done.40.got = bf16[24,6144]{1,0:T(8,128)(2,1)S(1)} collective-permute-done((bf16[24,6144]{1,0:T(8,128)(2,1)S(1)}, bf16[24,6144]{1,0:T(8,128)(2,1)S(1)}, u32[]{:S(2)}, u32[]{:S(2)}) %collective-permute-start.40) | collective-permute-done | bytes 294944 | tf_op jit(solution)/shard_map/ppermute | solution.py:708
  274.5 1.3 collective-permute-start.41
  275.8 2.2 collective-permute-start.42
  278.0 1.4 collective-permute-start.43
  279.4 2.8 collective-permute-done.44.refs_1_
  282.8 3.6 %collective-permute-start.45 = (bf16[24,3072]{1,0:T(8,128)(2,1)S(1)}, bf16[24,3072]{1,0:T(8,128)(2,1)S(1)}, u32[]{:S(2)}, u32[]{:S(2)}) collective-permute-start(bf16[24,3072]{1,0:T(8,128)(2,1)S(1)} %get-tuple-element.218), channel_id=1, source_target_pairs={{0,4},{1,5},{2,6},{3,7},{4,0},{5,1},{6,2},{7,3},{8,12},{9,13},{10,... | collective-permute-start | bytes 442376 | tf_op jit(solution)/shard_map/ppermute | solution.py:708
  288.5 3.3 %collective-permute-done.45.got = bf16[24,3072]{1,0:T(8,128)(2,1)S(1)} collective-permute-done((bf16[24,3072]{1,0:T(8,128)(2,1)S(1)}, bf16[24,3072]{1,0:T(8,128)(2,1)S(1)}, u32[]{:S(2)}, u32[]{:S(2)}) %collective-permute-start.45) | collective-permute-done | bytes 147488 | tf_op jit(solution)/shard_map/ppermute | solution.py:708
  (150 shorter events, 38.4 us)
Async XLA Ops:
  3.9 1.6 collective-permute-start.1
  4.4 7.0 %collective-permute-start = (bf16[24,3456]{1,0:T(8,128)(2,1)}, bf16[24,3456]{1,0:T(8,128)(2,1)S(1)}, u32[]{:S(2)}, u32[]{:S(2)}) collective-permute-start(bf16[24,3456]{1,0:T(8,128)(2,1)} %get-tuple-element.119), channel_id=1, source_target_pairs={{0,1},{1,0},{2,3},{3,2},{4,5},{5,4},{6,7},{7,6},{8,9},{9,8},{10,11... | collective-permute-start | bytes 497672 | tf_op jit(solution)/shard_map/ppermute | solution.py:708
  6.5 10.3 %collective-permute-start.2 = (bf16[48,1280]{1,0:T(8,128)(2,1)S(1)}, bf16[48,1280]{1,0:T(8,128)(2,1)S(1)}, u32[]{:S(2)}, u32[]{:S(2)}) collective-permute-start(bf16[48,1280]{1,0:T(8,128)(2,1)S(1)} %maximum_select_fusion.2), channel_id=1, source_target_pairs={{0,4},{1,5},{2,6},{3,7},{4,0},{5,1},{6,2},{7,3},{8,12},{9,13},{10,... | collective-permute-start | bytes 368648 | tf_op jit(solution)/shard_map/ppermute | solution.py:708
  16.8 7.6 %collective-permute-start.3 = (bf16[2,48,1280]{2,1,0:T(8,128)(2,1)S(1)}, bf16[2,48,1280]{2,1,0:T(8,128)(2,1)S(1)}, u32[]{:S(2)}, u32[]{:S(2)}) collective-permute-start(bf16[2,48,1280]{2,1,0:T(8,128)(2,1)S(1)} %pad_maximum_fusion.8), channel_id=1, source_target_pairs={{0,2},{1,3},{2,0},{3,1},{4,6},{5,7},{6,4},{7,5},{8,10},{9,11},{10,... | collective-permute-start | bytes 737288 | tf_op jit(solution)/shard_map/ppermute | solution.py:708
  24.4 6.7 %collective-permute-start.6 = (bf16[2,2,48,640]{3,2,1,0:T(8,128)(2,1)S(1)}, bf16[2,2,48,640]{3,2,1,0:T(8,128)(2,1)S(1)}, u32[]{:S(2)}, u32[]{:S(2)}) collective-permute-start(bf16[2,2,48,640]{3,2,1,0:T(8,128)(2,1)S(1)} %get-tuple-element.226), channel_id=1, source_target_pairs={{0,16},{1,17},{2,18},{3,19},{4,20},{5,21},{6,22},{7,23},{8,24},{9,... | collective-permute-start | bytes 737288 | tf_op jit(solution)/shard_map/ppermute | solution.py:708
  25.7 6.4 %collective-permute-start.5 = (bf16[2,2,48,640]{3,2,1,0:T(8,128)(2,1)S(1)}, bf16[2,2,48,640]{3,2,1,0:T(8,128)(2,1)S(1)}, u32[]{:S(2)}, u32[]{:S(2)}) collective-permute-start(bf16[2,2,48,640]{3,2,1,0:T(8,128)(2,1)S(1)} %get-tuple-element.227), channel_id=1, source_target_pairs={{0,8},{1,9},{2,10},{3,11},{4,12},{5,13},{6,14},{7,15},{8,0},{9,1},... | collective-permute-start | bytes 737288 | tf_op jit(solution)/shard_map/ppermute | solution.py:708
  27.2 17.0 %collective-permute-start.4 = (bf16[48,3456]{1,0:T(8,128)(2,1)S(1)}, bf16[48,3456]{1,0:T(8,128)(2,1)S(1)}, u32[]{:S(2)}, u32[]{:S(2)}) collective-permute-start(bf16[48,3456]{1,0:T(8,128)(2,1)S(1)} %maximum_select_fusion), channel_id=1, source_target_pairs={{0,4},{1,5},{2,6},{3,7},{4,0},{5,1},{6,2},{7,3},{8,12},{9,13},{10,... | collective-permute-start | bytes 995336 | tf_op jit(solution)/shard_map/ppermute | solution.py:708
  31.1 15.4 %collective-permute-start.11 = (bf16[2,2,2,48,640]{4,3,2,1,0:T(8,128)(2,1)S(1)}, bf16[2,2,2,48,640]{4,3,2,1,0:T(8,128)(2,1)S(1)}, u32[]{:S(2)}, u32[]{:S(2)}) collective-permute-start(bf16[2,2,2,48,640]{4,3,2,1,0:T(8,128)(2,1)S(1)} %pad_maximum_fusion.7), channel_id=1, source_target_pairs={{0,8},{1,9},{2,10},{3,11},{4,12},{5,13},{6,14},{7,15},{8,0},{9,1},... | collective-permute-start | bytes 1474568 | tf_op jit(solution)/shard_map/ppermute | solution.py:708
  32.2 15.0 %collective-permute-start.10 = (bf16[2,2,2,48,640]{4,3,2,1,0:T(8,128)(2,1)S(1)}, bf16[2,2,2,48,640]{4,3,2,1,0:T(8,128)(2,1)S(1)}, u32[]{:S(2)}, u32[]{:S(2)}) collective-permute-start(bf16[2,2,2,48,640]{4,3,2,1,0:T(8,128)(2,1)S(1)} %pad_maximum_fusion.6), channel_id=1, source_target_pairs={{0,16},{1,17},{2,18},{3,19},{4,20},{5,21},{6,22},{7,23},{8,24},{9,... | collective-permute-start | bytes 1474568 | tf_op jit(solution)/shard_map/ppermute | solution.py:708
  44.3 10.5 %collective-permute-start.9 = (bf16[2,48,1664]{2,1,0:T(8,128)(2,1)S(1)}, bf16[2,48,1664]{2,1,0:T(8,128)(2,1)S(1)}, u32[]{:S(2)}, u32[]{:S(2)}) collective-permute-start(bf16[2,48,1664]{2,1,0:T(8,128)(2,1)S(1)} %fusion.1), channel_id=1, source_target_pairs={{0,2},{1,3},{2,0},{3,1},{4,6},{5,7},{6,4},{7,5},{8,10},{9,11},{10,... | collective-permute-start | bytes 958472 | tf_op jit(solution)/shard_map/ppermute | solution.py:708
  45.1 15.2 %collective-permute-start.7 = (bf16[2,48,1792]{2,1,0:T(8,128)(2,1)S(1)}, bf16[2,48,1792]{2,1,0:T(8,128)(2,1)S(1)}, u32[]{:S(2)}, u32[]{:S(2)}) collective-permute-start(bf16[2,48,1792]{2,1,0:T(8,128)(2,1)S(1)} %fusion), channel_id=1, source_target_pairs={{0,2},{1,3},{2,0},{3,1},{4,6},{5,7},{6,4},{7,5},{8,10},{9,11},{10,... | collective-permute-start | bytes 1032200 | tf_op jit(solution)/shard_map/ppermute | solution.py:708
  46.5 14.4 %collective-permute-start.14 = (bf16[8,48,640]{2,1,0:T(8,128)(2,1)S(1)}, bf16[8,48,640]{2,1,0:T(8,128)(2,1)S(1)}, u32[]{:S(2)}, u32[]{:S(2)}) collective-permute-start(bf16[8,48,640]{2,1,0:T(8,128)(2,1)S(1)} %bitcast.113), channel_id=1, source_target_pairs={{0,1},{1,0},{2,3},{3,2},{4,5},{5,4},{6,7},{7,6},{8,9},{9,8},{10,11... | collective-permute-start | bytes 1474568 | tf_op jit(solution)/shard_map/ppermute | solution.py:708
  46.6 14.9 %collective-permute-start.12 = (bf16[8,48,640]{2,1,0:T(8,128)(2,1)S(1)}, bf16[8,48,640]{2,1,0:T(8,128)(2,1)S(1)}, u32[]{:S(2)}, u32[]{:S(2)}) collective-permute-start(bf16[8,48,640]{2,1,0:T(8,128)(2,1)S(1)} %bitcast.115), channel_id=1, source_target_pairs={{0,1},{1,0},{2,3},{3,2},{4,5},{5,4},{6,7},{7,6},{8,9},{9,8},{10,11... | collective-permute-start | bytes 1474568 | tf_op jit(solution)/shard_map/ppermute | solution.py:708
  47.1 14.4 %collective-permute-start.15 = (bf16[8,48,640]{2,1,0:T(8,128)(2,1)S(1)}, bf16[8,48,640]{2,1,0:T(8,128)(2,1)S(1)}, u32[]{:S(2)}, u32[]{:S(2)}) collective-permute-start(bf16[8,48,640]{2,1,0:T(8,128)(2,1)S(1)} %bitcast.137), channel_id=1, source_target_pairs={{0,1},{1,0},{2,3},{3,2},{4,5},{5,4},{6,7},{7,6},{8,9},{9,8},{10,11... | collective-permute-start | bytes 1474568 | tf_op jit(solution)/shard_map/ppermute | solution.py:708
  54.8 8.3 %collective-permute-start.13 = (bf16[8,48,640]{2,1,0:T(8,128)(2,1)S(1)}, bf16[8,48,640]{2,1,0:T(8,128)(2,1)}, u32[]{:S(2)}, u32[]{:S(2)}) collective-permute-start(bf16[8,48,640]{2,1,0:T(8,128)(2,1)S(1)} %bitcast.139), channel_id=1, source_target_pairs={{0,1},{1,0},{2,3},{3,2},{4,5},{5,4},{6,7},{7,6},{8,9},{9,8},{10,11... | collective-permute-start | bytes 1474568 | tf_op jit(solution)/shard_map/ppermute | solution.py:708
  60.3 14.6 %collective-permute-start.16 = (bf16[2,2,48,1664]{3,2,1,0:T(8,128)(2,1)S(1)}, bf16[2,2,48,1664]{3,2,1,0:T(8,128)(2,1)}, u32[]{:S(2)}, u32[]{:S(2)}) collective-permute-start(bf16[2,2,48,1664]{3,2,1,0:T(8,128)(2,1)S(1)} %get-tuple-element.225), channel_id=1, source_target_pairs={{0,16},{1,17},{2,18},{3,19},{4,20},{5,21},{6,22},{7,23},{8,24},{9,... | collective-permute-start | bytes 1916936 | tf_op jit(solution)/shard_map/ppermute | solution.py:708
  60.9 15.8 %collective-permute-start.8 = (bf16[2,2,48,1792]{3,2,1,0:T(8,128)(2,1)S(1)}, bf16[2,2,48,1792]{3,2,1,0:T(8,128)(2,1)S(1)}, u32[]{:S(2)}, u32[]{:S(2)}) collective-permute-start(bf16[2,2,48,1792]{3,2,1,0:T(8,128)(2,1)S(1)} %get-tuple-element.223), channel_id=1, source_target_pairs={{0,8},{1,9},{2,10},{3,11},{4,12},{5,13},{6,14},{7,15},{8,0},{9,1},... | collective-permute-start | bytes 2064392 | tf_op jit(solution)/shard_map/ppermute | solution.py:708
  76.1 28.3 %copy-start.21 = (bf16[2,2,2,48,1664]{4,3,2,1,0:T(8,128)(2,1)}, bf16[2,2,2,48,1664]{4,3,2,1,0:T(8,128)(2,1)S(1)}, u32[]{:S(2)}) copy-start(bf16[2,2,2,48,1664]{4,3,2,1,0:T(8,128)(2,1)S(1)} %pad_maximum_fusion.1) | copy-start | bytes 3833860
  76.1 33.5 %collective-permute-start.20 = (bf16[2,2,2,48,1664]{4,3,2,1,0:T(8,128)(2,1)S(1)}, bf16[2,2,2,48,1664]{4,3,2,1,0:T(8,128)(2,1)}, u32[]{:S(2)}, u32[]{:S(2)}) collective-permute-start(bf16[2,2,2,48,1664]{4,3,2,1,0:T(8,128)(2,1)S(1)} %pad_maximum_fusion.1), channel_id=1, source_target_pairs={{0,8},{1,9},{2,10},{3,11},{4,12},{5,13},{6,14},{7,15},{8,0},{9,1},... | collective-permute-start | bytes 3833864 | tf_op jit(solution)/shard_map/ppermute | solution.py:708
  76.7 27.7 %collective-permute-start.19 = (bf16[8,48,1664]{2,1,0:T(8,128)(2,1)S(1)}, bf16[8,48,1664]{2,1,0:T(8,128)(2,1)}, u32[]{:S(2)}, u32[]{:S(2)}) collective-permute-start(bf16[8,48,1664]{2,1,0:T(8,128)(2,1)S(1)} %bitcast.107), channel_id=1, source_target_pairs={{0,1},{1,0},{2,3},{3,2},{4,5},{5,4},{6,7},{7,6},{8,9},{9,8},{10,11... | collective-permute-start | bytes 3833864 | tf_op jit(solution)/shard_map/ppermute | solution.py:708
  76.8 27.5 %copy-start.20 = (bf16[2,2,2,48,1792]{4,3,2,1,0:T(8,128)(2,1)}, bf16[2,2,2,48,1792]{4,3,2,1,0:T(8,128)(2,1)S(1)}, u32[]{:S(2)}) copy-start(bf16[2,2,2,48,1792]{4,3,2,1,0:T(8,128)(2,1)S(1)} %pad_maximum_fusion) | copy-start | bytes 4128772
  76.8 32.8 %collective-permute-start.17 = (bf16[2,2,2,48,1792]{4,3,2,1,0:T(8,128)(2,1)S(1)}, bf16[2,2,2,48,1792]{4,3,2,1,0:T(8,128)(2,1)}, u32[]{:S(2)}, u32[]{:S(2)}) collective-permute-start(bf16[2,2,2,48,1792]{4,3,2,1,0:T(8,128)(2,1)S(1)} %pad_maximum_fusion), channel_id=1, source_target_pairs={{0,16},{1,17},{2,18},{3,19},{4,20},{5,21},{6,22},{7,23},{8,24},{9,... | collective-permute-start | bytes 4128776 | tf_op jit(solution)/shard_map/ppermute | solution.py:708
  79.1 25.3 %collective-permute-start.18 = (bf16[8,48,1792]{2,1,0:T(8,128)(2,1)S(1)}, bf16[8,48,1792]{2,1,0:T(8,128)(2,1)}, u32[]{:S(2)}, u32[]{:S(2)}) collective-permute-start(bf16[8,48,1792]{2,1,0:T(8,128)(2,1)S(1)} %bitcast.105), channel_id=1, source_target_pairs={{0,1},{1,0},{2,3},{3,2},{4,5},{5,4},{6,7},{7,6},{8,9},{9,8},{10,11... | collective-permute-start | bytes 4128776 | tf_op jit(solution)/shard_map/ppermute | solution.py:708
  109.6 5.2 %collective-permute-start.21 = (bf16[8,48,1792]{2,1,0:T(8,128)(2,1)}, bf16[8,48,1792]{2,1,0:T(8,128)(2,1)S(1)}, u32[]{:S(2)}, u32[]{:S(2)}) collective-permute-start(bf16[8,48,1792]{2,1,0:T(8,128)(2,1)} %bitcast.41.rest_1_), channel_id=1, source_target_pairs={{0,1},{1,0},{2,3},{3,2},{4,5},{5,4},{6,7},{7,6},{8,9},{9,8},{10,11... | collective-permute-start | bytes 4128776 | tf_op jit(solution)/shard_map/ppermute | solution.py:708
  109.6 5.2 %collective-permute-start.22 = (bf16[8,48,1664]{2,1,0:T(8,128)(2,1)}, bf16[8,48,1664]{2,1,0:T(8,128)(2,1)S(1)}, u32[]{:S(2)}, u32[]{:S(2)}) collective-permute-start(bf16[8,48,1664]{2,1,0:T(8,128)(2,1)} %bitcast.42.rest_3_), channel_id=1, source_target_pairs={{0,1},{1,0},{2,3},{3,2},{4,5},{5,4},{6,7},{7,6},{8,9},{9,8},{10,11... | collective-permute-start | bytes 3833864 | tf_op jit(solution)/shard_map/ppermute | solution.py:708
  162.9 9.9 %collective-permute-start.23 = (bf16[16,24,3072]{2,1,0:T(8,128)(2,1)}, bf16[16,24,3072]{2,1,0:T(8,128)(2,1)S(1)}, u32[]{:S(2)}, u32[]{:S(2)}) collective-permute-start(bf16[16,24,3072]{2,1,0:T(8,128)(2,1)} %get-tuple-element.149), channel_id=1, source_target_pairs={{0,1},{1,0},{2,3},{3,2},{4,5},{5,4},{6,7},{7,6},{8,9},{9,8},{10,11... | collective-permute-start | bytes 7077896 | tf_op jit(solution)/shard_map/ppermute | solution.py:708
  172.4 4.7 %collective-permute-start.24 = (bf16[16,24,3072]{2,1,0:T(8,128)(2,1)}, bf16[16,24,3072]{2,1,0:T(8,128)(2,1)S(1)}, u32[]{:S(2)}, u32[]{:S(2)}) collective-permute-start(bf16[16,24,3072]{2,1,0:T(8,128)(2,1)} %get-tuple-element.152), channel_id=1, source_target_pairs={{0,1},{1,0},{2,3},{3,2},{4,5},{5,4},{6,7},{7,6},{8,9},{9,8},{10,11... | collective-permute-start | bytes 7077896 | tf_op jit(solution)/shard_map/ppermute | solution.py:708
  180.9 29.3 %collective-permute-start.26 = (bf16[2,4,24,3072]{3,2,1,0:T(8,128)(2,1)}, bf16[2,4,24,3072]{3,2,1,0:T(8,128)(2,1)S(1)}, u32[]{:S(2)}, u32[]{:S(2)}) collective-permute-start(bf16[2,4,24,3072]{3,2,1,0:T(8,128)(2,1)} %get-tuple-element.169), channel_id=1, source_target_pairs={{0,16},{1,17},{2,18},{3,19},{4,20},{5,21},{6,22},{7,23},{8,24},{9,... | collective-permute-start | bytes 3538952 | tf_op jit(solution)/shard_map/ppermute | solution.py:708
  183.4 28.0 %collective-permute-start.25 = (bf16[2,4,24,3072]{3,2,1,0:T(8,128)(2,1)S(1)}, bf16[2,4,24,3072]{3,2,1,0:T(8,128)(2,1)S(1)}, u32[]{:S(2)}, u32[]{:S(2)}) collective-permute-start(bf16[2,4,24,3072]{3,2,1,0:T(8,128)(2,1)S(1)} %get-tuple-element.168), channel_id=1, source_target_pairs={{0,8},{1,9},{2,10},{3,11},{4,12},{5,13},{6,14},{7,15},{8,0},{9,1},... | collective-permute-start | bytes 3538952 | tf_op jit(solution)/shard_map/ppermute | solution.py:708
  217.0 14.5 %collective-permute-start.27 = (bf16[4,24,3072]{2,1,0:T(8,128)(2,1)S(1)}, bf16[4,24,3072]{2,1,0:T(8,128)(2,1)S(1)}, u32[]{:S(2)}, u32[]{:S(2)}) collective-permute-start(bf16[4,24,3072]{2,1,0:T(8,128)(2,1)S(1)} %get-tuple-element.176), channel_id=1, source_target_pairs={{0,16},{1,17},{2,18},{3,19},{4,20},{5,21},{6,22},{7,23},{8,24},{9,... | collective-permute-start | bytes 1769480 | tf_op jit(solution)/shard_map/ppermute | solution.py:708
  217.5 14.5 %collective-permute-start.28 = (bf16[4,24,3072]{2,1,0:T(8,128)(2,1)S(1)}, bf16[4,24,3072]{2,1,0:T(8,128)(2,1)S(1)}, u32[]{:S(2)}, u32[]{:S(2)}) collective-permute-start(bf16[4,24,3072]{2,1,0:T(8,128)(2,1)S(1)} %get-tuple-element.178), channel_id=1, source_target_pairs={{0,8},{1,9},{2,10},{3,11},{4,12},{5,13},{6,14},{7,15},{8,0},{9,1},... | collective-permute-start | bytes 1769480 | tf_op jit(solution)/shard_map/ppermute | solution.py:708
  228.6 8.1 %collective-permute-start.29 = (bf16[16,24,1536]{2,1,0:T(8,128)(2,1)}, bf16[16,24,1536]{2,1,0:T(8,128)(2,1)S(1)}, u32[]{:S(2)}, u32[]{:S(2)}) collective-permute-start(bf16[16,24,1536]{2,1,0:T(8,128)(2,1)} %get-tuple-element.181), channel_id=1, source_target_pairs={{0,1},{1,0},{2,3},{3,2},{4,5},{5,4},{6,7},{7,6},{8,9},{9,8},{10,11... | collective-permute-start | bytes 3538952 | tf_op jit(solution)/shard_map/ppermute | solution.py:708
  228.7 8.1 %collective-permute-start.30 = (bf16[16,24,1536]{2,1,0:T(8,128)(2,1)}, bf16[16,24,1536]{2,1,0:T(8,128)(2,1)S(1)}, u32[]{:S(2)}, u32[]{:S(2)}) collective-permute-start(bf16[16,24,1536]{2,1,0:T(8,128)(2,1)} %get-tuple-element.183), channel_id=1, source_target_pairs={{0,1},{1,0},{2,3},{3,2},{4,5},{5,4},{6,7},{7,6},{8,9},{9,8},{10,11... | collective-permute-start | bytes 3538952 | tf_op jit(solution)/shard_map/ppermute | solution.py:708
  234.8 18.0 %collective-permute-start.32 = (bf16[2,24,6144]{2,1,0:T(8,128)(2,1)S(1)}, bf16[2,24,6144]{2,1,0:T(8,128)(2,1)S(1)}, u32[]{:S(2)}, u32[]{:S(2)}) collective-permute-start(bf16[2,24,6144]{2,1,0:T(8,128)(2,1)S(1)} %get-tuple-element.194), channel_id=1, source_target_pairs={{0,2},{1,3},{2,0},{3,1},{4,6},{5,7},{6,4},{7,5},{8,10},{9,11},{10,... | collective-permute-start | bytes 1769480 | tf_op jit(solution)/shard_map/ppermute | solution.py:708
  240.1 14.5 %collective-permute-start.33 = (bf16[2,4,24,1536]{3,2,1,0:T(8,128)(2,1)S(1)}, bf16[2,4,24,1536]{3,2,1,0:T(8,128)(2,1)S(1)}, u32[]{:S(2)}, u32[]{:S(2)}) collective-permute-start(bf16[2,4,24,1536]{3,2,1,0:T(8,128)(2,1)S(1)} %get-tuple-element.197), channel_id=1, source_target_pairs={{0,8},{1,9},{2,10},{3,11},{4,12},{5,13},{6,14},{7,15},{8,0},{9,1},... | collective-permute-start | bytes 1769480 | tf_op jit(solution)/shard_map/ppermute | solution.py:708
  240.7 13.9 %collective-permute-start.34 = (bf16[2,4,24,1536]{3,2,1,0:T(8,128)(2,1)S(1)}, bf16[2,4,24,1536]{3,2,1,0:T(8,128)(2,1)S(1)}, u32[]{:S(2)}, u32[]{:S(2)}) collective-permute-start(bf16[2,4,24,1536]{3,2,1,0:T(8,128)(2,1)S(1)} %get-tuple-element.199), channel_id=1, source_target_pairs={{0,16},{1,17},{2,18},{3,19},{4,20},{5,21},{6,22},{7,23},{8,24},{9,... | collective-permute-start | bytes 1769480 | tf_op jit(solution)/shard_map/ppermute | solution.py:708
  255.8 10.0 %collective-permute-start.38 = (bf16[4,24,1536]{2,1,0:T(8,128)(2,1)S(1)}, bf16[4,24,1536]{2,1,0:T(8,128)(2,1)S(1)}, u32[]{:S(2)}, u32[]{:S(2)}) collective-permute-start(bf16[4,24,1536]{2,1,0:T(8,128)(2,1)S(1)} %get-tuple-element.202), channel_id=1, source_target_pairs={{0,16},{1,17},{2,18},{3,19},{4,20},{5,21},{6,22},{7,23},{8,24},{9,... | collective-permute-start | bytes 884744 | tf_op jit(solution)/shard_map/ppermute | solution.py:708
  256.7 9.7 %collective-permute-start.39 = (bf16[4,24,1536]{2,1,0:T(8,128)(2,1)S(1)}, bf16[4,24,1536]{2,1,0:T(8,128)(2,1)S(1)}, u32[]{:S(2)}, u32[]{:S(2)}) collective-permute-start(bf16[4,24,1536]{2,1,0:T(8,128)(2,1)S(1)} %get-tuple-element.203), channel_id=1, source_target_pairs={{0,8},{1,9},{2,10},{3,11},{4,12},{5,13},{6,14},{7,15},{8,0},{9,1},... | collective-permute-start | bytes 884744 | tf_op jit(solution)/shard_map/ppermute | solution.py:708
  258.1 14.0 %collective-permute-start.40 = (bf16[24,6144]{1,0:T(8,128)(2,1)S(1)}, bf16[24,6144]{1,0:T(8,128)(2,1)S(1)}, u32[]{:S(2)}, u32[]{:S(2)}) collective-permute-start(bf16[24,6144]{1,0:T(8,128)(2,1)S(1)} %get-tuple-element.205), channel_id=1, source_target_pairs={{0,4},{1,5},{2,6},{3,7},{4,0},{5,1},{6,2},{7,3},{8,12},{9,13},{10,... | collective-permute-start | bytes 884744 | tf_op jit(solution)/shard_map/ppermute | solution.py:708
  261.5 1.2 collective-permute-start.31
  262.8 10.2 %collective-permute-start.35 = (f32[1,9984]{1,0:T(1,128)S(1)}, f32[1,9984]{1,0:T(1,128)S(1)}, u32[]{:S(2)}, u32[]{:S(2)}) collective-permute-start(f32[1,9984]{1,0:T(1,128)S(1)} %add.63), channel_id=1, source_target_pairs={{0,8},{1,9},{2,10},{3,11},{4,12},{5,13},{6,14},{7,15},{8,0},{9,1},... | collective-permute-start | bytes 119816 | tf_op jit(solution)/shard_map/ppermute | solution.py:708
  264.6 8.4 %collective-permute-start.36 = (f32[1,9984]{1,0:T(1,128)S(1)}, f32[1,9984]{1,0:T(1,128)S(1)}, u32[]{:S(2)}, u32[]{:S(2)}) collective-permute-start(f32[1,9984]{1,0:T(1,128)S(1)} %add.63), channel_id=1, source_target_pairs={{0,16},{1,17},{2,18},{3,19},{4,20},{5,21},{6,22},{7,23},{8,24},{9,... | collective-permute-start | bytes 119816 | tf_op jit(solution)/shard_map/ppermute | solution.py:708
  265.8 7.1 %collective-permute-start.37 = (f32[1,9984]{1,0:T(1,128)S(1)}, f32[1,9984]{1,0:T(1,128)S(1)}, u32[]{:S(2)}, u32[]{:S(2)}) collective-permute-start(f32[1,9984]{1,0:T(1,128)S(1)} %add.63), channel_id=1, source_target_pairs={{0,24},{1,25},{2,26},{3,27},{4,28},{5,29},{6,30},{7,31},{8,16},{9,... | collective-permute-start | bytes 119816 | tf_op jit(solution)/shard_map/ppermute | solution.py:708
  273.7 8.5 %collective-permute-start.44 = (bf16[2,24,3072]{2,1,0:T(8,128)(2,1)S(1)}, bf16[2,24,3072]{2,1,0:T(8,128)(2,1)S(1)}, u32[]{:S(2)}, u32[]{:S(2)}) collective-permute-start(bf16[2,24,3072]{2,1,0:T(8,128)(2,1)S(1)} %get-tuple-element.213), channel_id=1, source_target_pairs={{0,2},{1,3},{2,0},{3,1},{4,6},{5,7},{6,4},{7,5},{8,10},{9,11},{10,... | collective-permute-start | bytes 884744 | tf_op jit(solution)/shard_map/ppermute | solution.py:708
  274.5 11.9 %collective-permute-start.41 = (f32[1,9984]{1,0:T(1,128)S(1)}, f32[1,9984]{1,0:T(1,128)S(1)}, u32[]{:S(2)}, u32[]{:S(2)}) collective-permute-start(f32[1,9984]{1,0:T(1,128)S(1)} %add_add_fusion.1), channel_id=1, source_target_pairs={{0,2},{1,3},{2,0},{3,1},{4,6},{5,7},{6,4},{7,5},{8,10},{9,11},{10,... | collective-permute-start | bytes 119816 | tf_op jit(solution)/shard_map/ppermute | solution.py:708
  275.8 10.6 %collective-permute-start.42 = (f32[1,9984]{1,0:T(1,128)S(1)}, f32[1,9984]{1,0:T(1,128)S(1)}, u32[]{:S(2)}, u32[]{:S(2)}) collective-permute-start(f32[1,9984]{1,0:T(1,128)S(1)} %add_add_fusion.1), channel_id=1, source_target_pairs={{0,4},{1,5},{2,6},{3,7},{4,0},{5,1},{6,2},{7,3},{8,12},{9,13},{10,... | collective-permute-start | bytes 119816 | tf_op jit(solution)/shard_map/ppermute | solution.py:708
  278.0 8.6 %collective-permute-start.43 = (f32[1,9984]{1,0:T(1,128)S(1)}, f32[1,9984]{1,0:T(1,128)S(1)}, u32[]{:S(2)}, u32[]{:S(2)}) collective-permute-start(f32[1,9984]{1,0:T(1,128)S(1)} %add_add_fusion.1), channel_id=1, source_target_pairs={{0,6},{1,7},{2,4},{3,5},{4,2},{5,3},{6,0},{7,1},{8,14},{9,15},{10,... | collective-permute-start | bytes 119816 | tf_op jit(solution)/shard_map/ppermute | solution.py:708
  282.8 9.0 %collective-permute-start.45 = (bf16[24,3072]{1,0:T(8,128)(2,1)S(1)}, bf16[24,3072]{1,0:T(8,128)(2,1)S(1)}, u32[]{:S(2)}, u32[]{:S(2)}) collective-permute-start(bf16[24,3072]{1,0:T(8,128)(2,1)S(1)} %get-tuple-element.218), channel_id=1, source_target_pairs={{0,4},{1,5},{2,6},{3,7},{4,0},{5,1},{6,2},{7,3},{8,12},{9,13},{10,... | collective-permute-start | bytes 442376 | tf_op jit(solution)/shard_map/ppermute | solution.py:708
  (30 other events, 142.3 us)
where the time goes:
time: 298 us; the launch traced here: 293 us
  Pallas kernels  150 us (50%)
  waiting for transfers between devices  70.1 us (24%)
  starting transfers between devices  48 us (16%)
  local copies, waits for them, and re-layouts  18 us (6%)
  other arithmetic  4.97 us (2%)
    ppermute x46, waiting for transfers between devices, permute(): return lax.ppermute(x, AXES, [(i, i ^ mask) for i in range(n)])  70.1 us
    ppermute x46, starting transfers between devices, permute(): return lax.ppermute(x, AXES, [(i, i ^ mask) for i in range(n)])  48 us
    pallas_call x1, Pallas kernels, ffn_call(): pl.pallas_call(functools.partial(ffn_kernel, rb=rb, n=n, nu=nu, pieces=le...  37.3 us
    pallas_call x1, Pallas kernels, attention_forward(): pl.pallas_call(functools.partial(fwd_kernel, qb=qb, nq=nq, rc=32), grid=(...  25.2 us
    pallas_call x1, Pallas kernels, attention_backward(): pl.pallas_call(functools.partial(bwd_kernel, qb=qb, nq=nq, rc=64), grid=(...  21.1 us
    unnamed x64, local copies, waits for them, and re-layouts  15.7 us
    pallas_call x9, Pallas kernels, fold(): pl.pallas_call(functools.partial(fold_kernel, plan=plan, joined=joined),...  11.3 us
    pallas_call x1, Pallas kernels, first_backward(): pl.pallas_call(first_kernel, grid=(s // rb,), in_specs=[row(d), row(d), p...  10.8 us
  transfers between devices with their start and end apart: 46, of which 20 were waited for; matrix products, arithmetic and copies ran while one was open for 2% of the time, Pallas kernels for 32%

commit v1 on v0

--- a/solution.py
+++ b/solution.py
@@ -379,7 +379,7 @@
             pltpu.VMEM((2, 128, qb), bf16),
             pltpu.VMEM((qb, 128), f32),
         ],
-        compiler_params=params(60),
+        compiler_params=params(40),
         cost_estimate=cost(26),
     )(tie(lens, *deps), qkv, qkv, qkv, o, rz, dol, *kept)
 
@@ -397,32 +397,36 @@
     def weight(at):
         return w_ref[:, :, at : at + d].reshape(d, d)
 
+    core = idx_ref[3]
+
+    def copies(k):
+        if pieces == 1:
+            return [pltpu.make_async_copy(parts[0], w_ref, sems.at[0])]
+        who, later, half = core if k < 4 else 1 - core, (k // 2) % 2, wide // 2
+        lane = pl.multiple_of(who * half + later * cut, 128)
+        size = half - cut if later else cut
+        return [
+            pltpu.make_async_copy(
+                parts[k].at[at], w_ref.at[gathered_chip(idx_ref, k, at), :, pl.ds(lane, size)], sems.at[k * 8 + at]
+            )
+            for at in range(8)
+        ]
+
+    def wait(which):
+        for k in which:
+            for copy in copies(k):
+                copy.wait()
+
+    order = (0, 1, 4, 5, 2, 3, 6, 7) if pieces > 1 else (0,)
+
     @pl.when(i == 0)
     def _():
-        if pieces == 1:
-            copies = [pltpu.make_async_copy(parts[0], w_ref, sems.at[0])]
-        else:
-            copies = []
-            half = wide // 2
-            core = idx_ref[3]
-            for k, part in enumerate(parts):
-                who, later = core if k < 4 else 1 - core, (k // 2) % 2
-                lane = pl.multiple_of(who * half + later * cut, 128)
-                for at in range(8):
-                    to = w_ref.at[gathered_chip(idx_ref, k, at), :, pl.ds(lane, half - cut if later else cut)]
-                    copies.append(pltpu.make_async_copy(part.at[at], to, sems.at[k * 8 + at]))
-        for copy in copies:
-            copy.start()
+        for k in order:
+            for copy in copies(k):
+                copy.start()
         for s in (sbd, sbu, sg2, sb2, sbo):
             s[...] = jnp.zeros_like(s)
-        for copy in copies:
-            copy.wait()
-        for dev in range(n):
-            for j in range(nu):
-                at = (dev * nu + j) * each
-                row = dev * each
-                lane = (1 + nu + j) * d
-                wd[at : at + each, :] = w_ref[row // rows, row % rows : row % rows + each, lane : lane + d]
+        wait(order[:4])
 
     live = (lax.broadcasted_iota(jnp.int32, (rb, 1), 0) + i * rb) < len_ref[0]
     r = x_ref[...].astype(f32) + dot(o_ref[...], weight(0), NN) + bo_ref[...]
@@ -434,6 +438,17 @@
     dyl_ref[...] = dyl
     y = r + bd_ref[...]
     dc = jnp.zeros_like(r)
+
+    @pl.when(i == 0)
+    def _():
+        wait(order[4:])
+        for dev in range(n):
+            for j in range(nu):
+                at = (dev * nu + j) * each
+                row = dev * each
+                lane = (1 + nu + j) * d
+                wd[at : at + each, :] = w_ref[row // rows, row % rows : row % rows + each, lane : lane + d]
+
     k0 = math.sqrt(2 / math.pi)
     for j in range(nu):
         cols = slice(j * d, (j + 1) * d)
@@ -626,7 +641,7 @@
        ,
         out_specs=[spec_a, spec_a, spec_b, spec_b],
         out_shape=[sds((n // 2, each, 2 * d), bf16)] * 4,
-        compiler_params=params(60),
+        compiler_params=params(40),
         cost_estimate=cost(40),
     )(tie(idx, *deps), a, dqkv, o, drl)
 
@@ -680,7 +695,7 @@
        ,
         out_specs=[row(d), pl.BlockSpec((1, wide), lambda i: (0, 0))],
         out_shape=[sds((s, d), f32), sds((1, wide), f32)],
-        compiler_params=params(60),
+        compiler_params=params(40),
         cost_estimate=cost(10),
     )(x, dr, dqkv, w, tie(gain, *deps), *sums)
 

time: 298 us -> 285 us (0.956)
  Pallas kernels: 150 us -> 124 us
  waiting for transfers between devices: 70.1 us -> 92.9 us
  local copies, waits for them, and re-layouts: 18 us -> 10.3 us
    ppermute x46, waiting for transfers between devices: 70.1 us -> 92.9 us  [permute(): return lax.ppermute(x, AXES, [(i, i ^ mask) for i in range(n)])]
    pallas_call x1, Pallas kernels: 25.2 us -> 14.4 us  [attention_forward(): pl.pallas_call(functools.partial(fwd_kernel, qb=qb, nq=nq, rc=32), grid=(...]
    unnamed x64 -> x66, local copies, waits for them, and re-layouts: 15.7 us -> 7.91 us
    pallas_call x1, Pallas kernels: 21.1 us -> 14.1 us  [attention_backward(): pl.pallas_call(functools.partial(bwd_kernel, qb=qb, nq=nq, rc=64), grid=(...]
    pallas_call x1, Pallas kernels: 10.7 us -> 6.85 us  [attention_grads(): pl.pallas_call(functools.partial(attention_grads_kernel, each=each), grid...]
  transfers between devices with their start and end apart: 46 -> 46, of which waited for: 20 -> 22; matrix products, arithmetic and copies ran while one was open for 2% -> 2% of each run, Pallas kernels for 32% -> 25%
where the time goes in v1:
time: 285 us; the launch traced here: 280 us
  Pallas kernels  124 us (44%)
  waiting for transfers between devices  92.9 us (33%)
  starting transfers between devices  46.5 us (16%)
  local copies, waits for them, and re-layouts  10.3 us (4%)
  other arithmetic  4.97 us (2%)
    ppermute x46, waiting for transfers between devices, permute(): return lax.ppermute(x, AXES, [(i, i ^ mask) for i in range(n)])  92.9 us
    ppermute x46, starting transfers between devices, permute(): return lax.ppermute(x, AXES, [(i, i ^ mask) for i in range(n)])  46.5 us
    pallas_call x1, Pallas kernels, ffn_call(): pl.pallas_call(functools.partial(ffn_kernel, rb=rb, n=n, nu=nu, pieces=le...  37 us
    pallas_call x1, Pallas kernels, attention_forward(): pl.pallas_call(functools.partial(fwd_kernel, qb=qb, nq=nq, rc=32), grid=(...  14.4 us
    pallas_call x1, Pallas kernels, attention_backward(): pl.pallas_call(functools.partial(bwd_kernel, qb=qb, nq=nq, rc=64), grid=(...  14.1 us
    pallas_call x1, Pallas kernels, qkv_call(): pl.pallas_call(functools.partial(qkv_kernel, n=n, each=each, layout=layou...  10.3 us
    pallas_call x9, Pallas kernels, fold(): pl.pallas_call(functools.partial(fold_kernel, plan=plan, joined=joined),...  10.3 us
    pallas_call x1, Pallas kernels, down_grad(): pl.pallas_call(functools.partial(down_kernel, each=each, nu=nu), grid=(nu...  9.28 us
  transfers between devices with their start and end apart: 46, of which 22 were waited for; matrix products, arithmetic and copies ran while one was open for 2% of the time, Pallas kernels for 25%

profile of v1, /device:TPU:0, one launch (start us, length us, event | category | flops | bytes accessed | tf_op | source)
XLA Modules:
  0.0 280.4 jit_solution(18299807946109747955)
XLA Ops:
  1.3 2.6 shard_map.254
  6.5 4.0 %collective-permute-start.2 = (bf16[48,1280]{1,0:T(8,128)(2,1)S(1)}, bf16[48,1280]{1,0:T(8,128)(2,1)S(1)}, u32[]{:S(2)}, u32[]{:S(2)}) collective-permute-start(bf16[48,1280]{1,0:T(8,128)(2,1)S(1)} %maximum_select_fusion.2), channel_id=1, source_target_pairs={{0,4},{1,5},{2,6},{3,7},{4,0},{5,1},{6,2},{7,3},{8,12},{9,13},{10,... | collective-permute-start | bytes 368648 | tf_op jit(solution)/shard_map/ppermute | solution.py:723
  12.5 4.3 %collective-permute-done.2 = bf16[48,1280]{1,0:T(8,128)(2,1)S(1)} collective-permute-done((bf16[48,1280]{1,0:T(8,128)(2,1)S(1)}, bf16[48,1280]{1,0:T(8,128)(2,1)S(1)}, u32[]{:S(2)}, u32[]{:S(2)}) %collective-permute-start.2) | collective-permute-done | bytes 122912 | tf_op jit(solution)/shard_map/ppermute | solution.py:723
  17.6 6.8 %collective-permute-done.3 = bf16[2,48,1280]{2,1,0:T(8,128)(2,1)S(1)} collective-permute-done((bf16[2,48,1280]{2,1,0:T(8,128)(2,1)S(1)}, bf16[2,48,1280]{2,1,0:T(8,128)(2,1)S(1)}, u32[]{:S(2)}, u32[]{:S(2)}) %collective-permute-start.3) | collective-permute-done | bytes 245792 | tf_op jit(solution)/shard_map/ppermute | solution.py:723
  24.4 1.3 collective-permute-start.6
  25.7 1.5 collective-permute-start.5
  27.2 3.0 %collective-permute-start.4 = (bf16[48,3456]{1,0:T(8,128)(2,1)S(1)}, bf16[48,3456]{1,0:T(8,128)(2,1)S(1)}, u32[]{:S(2)}, u32[]{:S(2)}) collective-permute-start(bf16[48,3456]{1,0:T(8,128)(2,1)S(1)} %maximum_select_fusion), channel_id=1, source_target_pairs={{0,4},{1,5},{2,6},{3,7},{4,0},{5,1},{6,2},{7,3},{8,12},{9,13},{10,... | collective-permute-start | bytes 995336 | tf_op jit(solution)/shard_map/ppermute | solution.py:723
  32.2 1.6 collective-permute-start.10
  33.8 10.5 %collective-permute-done.4 = bf16[48,3456]{1,0:T(8,128)(2,1)S(1)} collective-permute-done((bf16[48,3456]{1,0:T(8,128)(2,1)S(1)}, bf16[48,3456]{1,0:T(8,128)(2,1)S(1)}, u32[]{:S(2)}, u32[]{:S(2)}) %collective-permute-start.4) | collective-permute-done | bytes 331808 | tf_op jit(solution)/shard_map/ppermute | solution.py:723
  45.1 1.4 collective-permute-start.7
  47.2 7.6 %collective-permute-done.9 = bf16[2,48,1664]{2,1,0:T(8,128)(2,1)S(1)} collective-permute-done((bf16[2,48,1664]{2,1,0:T(8,128)(2,1)S(1)}, bf16[2,48,1664]{2,1,0:T(8,128)(2,1)S(1)}, u32[]{:S(2)}, u32[]{:S(2)}) %collective-permute-start.9) | collective-permute-done | bytes 319520 | tf_op jit(solution)/shard_map/ppermute | solution.py:723
  55.0 5.3 %collective-permute-done.7 = bf16[2,48,1792]{2,1,0:T(8,128)(2,1)S(1)} collective-permute-done((bf16[2,48,1792]{2,1,0:T(8,128)(2,1)S(1)}, bf16[2,48,1792]{2,1,0:T(8,128)(2,1)S(1)}, u32[]{:S(2)}, u32[]{:S(2)}) %collective-permute-start.7) | collective-permute-done | bytes 344096 | tf_op jit(solution)/shard_map/ppermute | solution.py:723
  63.1 10.3 %shard_map.255 = (bf16[1024,768]{1,0:T(8,128)(2,1)}, bf16[1024,2304]{1,0:T(8,128)(2,1)}, bf16[4,16,48,640]{3,2,1,0:T(8,128)(2,1)}, f32[1,768]{1,0:T(1,128)}, f32...) custom-call(s32[6]{0:T(128)} %stack.27.idx_ref, ...), custom_call_target="tpu_custom_call" | custom-call | flops 8999999488 | tf_op jit(solution)/shard_map/pallas_call | solution.py:158
  73.4 1.5 collective-permute-done.16
  74.9 1.2 pad_maximum_fusion.1
  76.8 2.3 collective-permute-start.17
  79.1 14.4 %shard_map.256 = (bf16[1024,768]{1,0:T(8,128)(2,1)}, f32[1024,768]{1,0:T(8,128)}, bf16[12,256,256]{2,1,0:T(8,128)(2,1)}, bf16[12,256,512]{2,1,0:T(8,128)(2,1)}, ...) custom-call(s32[1]{0:T(128)S(6)} %copy.29.len_ref, ...), custom_call_target="tpu_custom_call" | custom-call | flops 44999999488 | tf_op jit(solution)/shard_map/pallas_call | solution.py:275
  93.6 16.0 %collective-permute-done.17 = bf16[2,2,2,48,1792]{4,3,2,1,0:T(8,128)(2,1)} collective-permute-done((bf16[2,2,2,48,1792]{4,3,2,1,0:T(8,128)(2,1)S(1)}, bf16[2,2,2,48,1792]{4,3,2,1,0:T(8,128)(2,1)}, u32[]{:S(2)}, u32[]{:S(2)}) %collective-permute-start.17) | collective-permute-done | bytes 1376288 | tf_op jit(solution)/shard_map/ppermute | solution.py:723
  110.1 4.7 %collective-permute-done.22.rest_7_ = bf16[8,48,1664]{2,1,0:T(8,128)(2,1)S(1)} collective-permute-done((bf16[8,48,1664]{2,1,0:T(8,128)(2,1)}, bf16[8,48,1664]{2,1,0:T(8,128)(2,1)S(1)}, u32[]{:S(2)}, u32[]{:S(2)}) %collective-permute-start.22) | collective-permute-done | bytes 1277984 | tf_op jit(solution)/shard_map/ppermute | solution.py:723
  116.2 37.0 %shard_map.257 = (bf16[1024,768]{1,0:T(8,128)(2,1)}, bf16[1024,3072]{1,0:T(8,128)(2,1)}, bf16[1024,3072]{1,0:T(8,128)(2,1)}, bf16[1024,768]{1,0:T(8,128)(2,1)}, ...) custom-call(s32[1]{0:T(128)S(6)} %copy.29.len_ref, ...), custom_call_target="tpu_custom_call" | custom-call | flops 36999999488 | tf_op jit(solution)/shard_map/pallas_call | solution.py:495
  153.2 9.3 %shard_map.259 = (bf16[16,24,3072]{2,1,0:T(8,128)(2,1)}, bf16[16,24,3072]{2,1,0:T(8,128)(2,1)}) custom-call(s32[6]{0:T(128)} %stack.27.idx_ref, bf16[1024,3072]{1,0:T(8,128)(2,1)} %get-tuple-element.146.g_ref, bf16[1024,768]{1,0:T(8,128)(2,1)} %get-tuple-element.147.b_ref), custom_call_target="tpu_custom_call" | custom-call | flops 8999999488 | tf_op jit(solution)/shard_map/pallas_call | solution.py:578
  162.6 9.3 %shard_map.258 = (bf16[16,24,3072]{2,1,0:T(8,128)(2,1)}, bf16[16,24,3072]{2,1,0:T(8,128)(2,1)}) custom-call(s32[6]{0:T(128)} %stack.27.idx_ref, bf16[1024,768]{1,0:T(8,128)(2,1)} %get-tuple-element.142.c_ref, bf16[1024,3072]{1,0:T(8,128)(2,1)} %get-tuple-element.143.du_ref), custom_call_target="tpu_custom_call" | custom-call | flops 8999999488 | tf_op jit(solution)/shard_map/pallas_call | solution.py:598
  172.3 1.7 copy-done.2
  173.9 1.6 shard_map.260
  176.6 1.6 shard_map.261
  180.4 14.1 %shard_map.262.dqkv_ref.dq_ref = bf16[3,1024,768]{2,1,0:T(8,128)(2,1)} custom-call(s32[1]{0:T(128)S(6)} %copy.29.len_ref, bf16[1024,2304]{1,0:T(8,128)(2,1)} %get-tuple-element.128.q_ref.k_ref.v_ref, bf16[1024,2304]{1,0:T(8,128)(2,1)} %get-tuple-element.128.q_ref.k_ref.v_ref, bf16[1024,2304]{1,0:T(8,128)(2,1)} %get-tuple-element.128.q_ref.k_ref.v_ref, ...), custom_call_target="tpu_custom_call" | custom-call | flops 25999998976 | tf_op jit(solution)/shard_map/pallas_call | solution.py:366
  194.5 12.1 %collective-permute-done.26.refs_3_ = bf16[2,4,24,3072]{3,2,1,0:T(8,128)(2,1)S(1)} collective-permute-done((bf16[2,4,24,3072]{3,2,1,0:T(8,128)(2,1)S(1)}, bf16[2,4,24,3072]{3,2,1,0:T(8,128)(2,1)S(1)}, u32[]{:S(2)}, u32[]{:S(2)}) %collective-permute-start.26) | collective-permute-done | bytes 1179680 | tf_op jit(solution)/shard_map/ppermute | solution.py:723
  207.3 1.5 shard_map.263
  209.9 1.5 collective-permute-start.28
  211.4 6.9 %shard_map.264 = (bf16[16,24,1536]{2,1,0:T(8,128)(2,1)S(1)}, bf16[16,24,1536]{2,1,0:T(8,128)(2,1)S(1)}, bf16[16,24,1536]{2,1,0:T(8,128)(2,1)S(1)}, bf16[16,24,1536]{2,1,0:T(8,128)(2,1)S(1)}) custom-call(s32[6]{0:T(128)S(1)} %copy-done, bf16[1024,768]{1,0:T(8,128)(2,1)S(1)} %copy-done.11, bf16[3,1024,768]{2,1,0:T(8,128)(2,1)S(1)} %copy-done.4, ...), custom_call_target="tpu_custom_call" | custom-call | flops 40000000000 | tf_op jit(solution)/shard_map/pallas_call | solution.py:631
  218.8 4.5 %collective-permute-done.27 = bf16[4,24,3072]{2,1,0:T(8,128)(2,1)S(1)} collective-permute-done((bf16[4,24,3072]{2,1,0:T(8,128)(2,1)S(1)}, bf16[4,24,3072]{2,1,0:T(8,128)(2,1)S(1)}, u32[]{:S(2)}, u32[]{:S(2)}) %collective-permute-start.27) | collective-permute-done | bytes 589856 | tf_op jit(solution)/shard_map/ppermute | solution.py:723
  224.9 3.9 %collective-permute-start.32 = (bf16[2,24,6144]{2,1,0:T(8,128)(2,1)S(1)}, bf16[2,24,6144]{2,1,0:T(8,128)(2,1)S(1)}, u32[]{:S(2)}, u32[]{:S(2)}) collective-permute-start(bf16[2,24,6144]{2,1,0:T(8,128)(2,1)S(1)} %get-tuple-element.194), channel_id=1, source_target_pairs={{0,2},{1,3},{2,0},{3,1},{4,6},{5,7},{6,4},{7,5},{8,10},{9,11},{10,... | collective-permute-start | bytes 1769480 | tf_op jit(solution)/shard_map/ppermute | solution.py:723
  228.9 1.6 shard_map.266
  232.4 2.3 copy-done.5
  234.8 7.9 %shard_map.267 = (f32[1024,768]{1,0:T(8,128)}, f32[1,9984]{1,0:T(1,128)S(1)}) custom-call(bf16[1024,768]{1,0:T(8,128)(2,1)S(1)} %bitcast.85, f32[1024,768]{1,0:T(8,128)S(1)} %copy-done.7, bf16[3,1024,768]{2,1,0:T(8,128)(2,1)S(1)} %copy-done.5, bf16[4,16,48,640]{3,2,1,0:T(8,128)(2,1)S(1)} %copy-done.6, f32[1,768]{1,0:T(1,128)S(1)} %copy-done.17, ...), custom_call_target="tpu_custom_call" | custom-call | flops 10000000000 | tf_op jit(solution)/shard_map/pallas_call | solution.py:690
  245.9 1.7 collective-permute-start.39
  247.5 3.1 %collective-permute-start.40 = (bf16[24,6144]{1,0:T(8,128)(2,1)S(1)}, bf16[24,6144]{1,0:T(8,128)(2,1)S(1)}, u32[]{:S(2)}, u32[]{:S(2)}) collective-permute-start(bf16[24,6144]{1,0:T(8,128)(2,1)S(1)} %get-tuple-element.205), channel_id=1, source_target_pairs={{0,4},{1,5},{2,6},{3,7},{4,0},{5,1},{6,2},{7,3},{8,12},{9,13},{10,... | collective-permute-start | bytes 884744 | tf_op jit(solution)/shard_map/ppermute | solution.py:723
  250.7 1.2 collective-permute-done.31
  251.9 1.2 collective-permute-start.35
  253.1 1.1 collective-permute-start.36
  254.2 1.3 collective-permute-start.37
  255.5 4.8 %collective-permute-done.40.got = bf16[24,6144]{1,0:T(8,128)(2,1)S(1)} collective-permute-done((bf16[24,6144]{1,0:T(8,128)(2,1)S(1)}, bf16[24,6144]{1,0:T(8,128)(2,1)S(1)}, u32[]{:S(2)}, u32[]{:S(2)}) %collective-permute-start.40) | collective-permute-done | bytes 294944 | tf_op jit(solution)/shard_map/ppermute | solution.py:723
  262.0 2.0 collective-permute-start.41
  264.0 1.3 collective-permute-start.42
  265.2 1.4 collective-permute-start.43
  266.6 4.7 %collective-permute-done.44.refs_1_ = bf16[2,24,3072]{2,1,0:T(8,128)(2,1)S(1)} collective-permute-done((bf16[2,24,3072]{2,1,0:T(8,128)(2,1)S(1)}, bf16[2,24,3072]{2,1,0:T(8,128)(2,1)S(1)}, u32[]{:S(2)}, u32[]{:S(2)}) %collective-permute-start.44) | collective-permute-done | bytes 294944 | tf_op jit(solution)/shard_map/ppermute | solution.py:723
  272.9 1.2 collective-permute-done.43
  276.0 3.2 %collective-permute-done.45.got = bf16[24,3072]{1,0:T(8,128)(2,1)S(1)} collective-permute-done((bf16[24,3072]{1,0:T(8,128)(2,1)S(1)}, bf16[24,3072]{1,0:T(8,128)(2,1)S(1)}, u32[]{:S(2)}, u32[]{:S(2)}) %collective-permute-start.45) | collective-permute-done | bytes 147488 | tf_op jit(solution)/shard_map/ppermute | solution.py:723
  (152 shorter events, 33.1 us)
Async XLA Ops:
  3.9 1.6 collective-permute-start.1
  4.4 7.0 %collective-permute-start = (bf16[24,3456]{1,0:T(8,128)(2,1)}, bf16[24,3456]{1,0:T(8,128)(2,1)S(1)}, u32[]{:S(2)}, u32[]{:S(2)}) collective-permute-start(bf16[24,3456]{1,0:T(8,128)(2,1)} %get-tuple-element.119), channel_id=1, source_target_pairs={{0,1},{1,0},{2,3},{3,2},{4,5},{5,4},{6,7},{7,6},{8,9},{9,8},{10,11... | collective-permute-start | bytes 497672 | tf_op jit(solution)/shard_map/ppermute | solution.py:723
  6.5 10.3 %collective-permute-start.2 = (bf16[48,1280]{1,0:T(8,128)(2,1)S(1)}, bf16[48,1280]{1,0:T(8,128)(2,1)S(1)}, u32[]{:S(2)}, u32[]{:S(2)}) collective-permute-start(bf16[48,1280]{1,0:T(8,128)(2,1)S(1)} %maximum_select_fusion.2), channel_id=1, source_target_pairs={{0,4},{1,5},{2,6},{3,7},{4,0},{5,1},{6,2},{7,3},{8,12},{9,13},{10,... | collective-permute-start | bytes 368648 | tf_op jit(solution)/shard_map/ppermute | solution.py:723
  16.8 7.6 %collective-permute-start.3 = (bf16[2,48,1280]{2,1,0:T(8,128)(2,1)S(1)}, bf16[2,48,1280]{2,1,0:T(8,128)(2,1)S(1)}, u32[]{:S(2)}, u32[]{:S(2)}) collective-permute-start(bf16[2,48,1280]{2,1,0:T(8,128)(2,1)S(1)} %pad_maximum_fusion.8), channel_id=1, source_target_pairs={{0,2},{1,3},{2,0},{3,1},{4,6},{5,7},{6,4},{7,5},{8,10},{9,11},{10,... | collective-permute-start | bytes 737288 | tf_op jit(solution)/shard_map/ppermute | solution.py:723
  24.4 6.7 %collective-permute-start.6 = (bf16[2,2,48,640]{3,2,1,0:T(8,128)(2,1)S(1)}, bf16[2,2,48,640]{3,2,1,0:T(8,128)(2,1)S(1)}, u32[]{:S(2)}, u32[]{:S(2)}) collective-permute-start(bf16[2,2,48,640]{3,2,1,0:T(8,128)(2,1)S(1)} %get-tuple-element.226), channel_id=1, source_target_pairs={{0,16},{1,17},{2,18},{3,19},{4,20},{5,21},{6,22},{7,23},{8,24},{9,... | collective-permute-start | bytes 737288 | tf_op jit(solution)/shard_map/ppermute | solution.py:723
  25.7 6.4 %collective-permute-start.5 = (bf16[2,2,48,640]{3,2,1,0:T(8,128)(2,1)S(1)}, bf16[2,2,48,640]{3,2,1,0:T(8,128)(2,1)S(1)}, u32[]{:S(2)}, u32[]{:S(2)}) collective-permute-start(bf16[2,2,48,640]{3,2,1,0:T(8,128)(2,1)S(1)} %get-tuple-element.227), channel_id=1, source_target_pairs={{0,8},{1,9},{2,10},{3,11},{4,12},{5,13},{6,14},{7,15},{8,0},{9,1},... | collective-permute-start | bytes 737288 | tf_op jit(solution)/shard_map/ppermute | solution.py:723
  27.2 17.0 %collective-permute-start.4 = (bf16[48,3456]{1,0:T(8,128)(2,1)S(1)}, bf16[48,3456]{1,0:T(8,128)(2,1)S(1)}, u32[]{:S(2)}, u32[]{:S(2)}) collective-permute-start(bf16[48,3456]{1,0:T(8,128)(2,1)S(1)} %maximum_select_fusion), channel_id=1, source_target_pairs={{0,4},{1,5},{2,6},{3,7},{4,0},{5,1},{6,2},{7,3},{8,12},{9,13},{10,... | collective-permute-start | bytes 995336 | tf_op jit(solution)/shard_map/ppermute | solution.py:723
  31.1 15.4 %collective-permute-start.11 = (bf16[2,2,2,48,640]{4,3,2,1,0:T(8,128)(2,1)S(1)}, bf16[2,2,2,48,640]{4,3,2,1,0:T(8,128)(2,1)S(1)}, u32[]{:S(2)}, u32[]{:S(2)}) collective-permute-start(bf16[2,2,2,48,640]{4,3,2,1,0:T(8,128)(2,1)S(1)} %pad_maximum_fusion.7), channel_id=1, source_target_pairs={{0,8},{1,9},{2,10},{3,11},{4,12},{5,13},{6,14},{7,15},{8,0},{9,1},... | collective-permute-start | bytes 1474568 | tf_op jit(solution)/shard_map/ppermute | solution.py:723
  32.2 22.7 %copy-start.25 = (bf16[2,2,2,48,640]{4,3,2,1,0:T(8,128)(2,1)}, bf16[2,2,2,48,640]{4,3,2,1,0:T(8,128)(2,1)S(1)}, u32[]{:S(2)}) copy-start(bf16[2,2,2,48,640]{4,3,2,1,0:T(8,128)(2,1)S(1)} %pad_maximum_fusion.6) | copy-start | bytes 1474564
  32.2 15.0 %collective-permute-start.10 = (bf16[2,2,2,48,640]{4,3,2,1,0:T(8,128)(2,1)S(1)}, bf16[2,2,2,48,640]{4,3,2,1,0:T(8,128)(2,1)S(1)}, u32[]{:S(2)}, u32[]{:S(2)}) collective-permute-start(bf16[2,2,2,48,640]{4,3,2,1,0:T(8,128)(2,1)S(1)} %pad_maximum_fusion.6), channel_id=1, source_target_pairs={{0,16},{1,17},{2,18},{3,19},{4,20},{5,21},{6,22},{7,23},{8,24},{9,... | collective-permute-start | bytes 1474568 | tf_op jit(solution)/shard_map/ppermute | solution.py:723
  44.3 10.5 %collective-permute-start.9 = (bf16[2,48,1664]{2,1,0:T(8,128)(2,1)S(1)}, bf16[2,48,1664]{2,1,0:T(8,128)(2,1)S(1)}, u32[]{:S(2)}, u32[]{:S(2)}) collective-permute-start(bf16[2,48,1664]{2,1,0:T(8,128)(2,1)S(1)} %fusion.1), channel_id=1, source_target_pairs={{0,2},{1,3},{2,0},{3,1},{4,6},{5,7},{6,4},{7,5},{8,10},{9,11},{10,... | collective-permute-start | bytes 958472 | tf_op jit(solution)/shard_map/ppermute | solution.py:723
  45.1 15.2 %collective-permute-start.7 = (bf16[2,48,1792]{2,1,0:T(8,128)(2,1)S(1)}, bf16[2,48,1792]{2,1,0:T(8,128)(2,1)S(1)}, u32[]{:S(2)}, u32[]{:S(2)}) collective-permute-start(bf16[2,48,1792]{2,1,0:T(8,128)(2,1)S(1)} %fusion), channel_id=1, source_target_pairs={{0,2},{1,3},{2,0},{3,1},{4,6},{5,7},{6,4},{7,5},{8,10},{9,11},{10,... | collective-permute-start | bytes 1032200 | tf_op jit(solution)/shard_map/ppermute | solution.py:723
  46.5 14.4 %collective-permute-start.14 = (bf16[8,48,640]{2,1,0:T(8,128)(2,1)S(1)}, bf16[8,48,640]{2,1,0:T(8,128)(2,1)S(1)}, u32[]{:S(2)}, u32[]{:S(2)}) collective-permute-start(bf16[8,48,640]{2,1,0:T(8,128)(2,1)S(1)} %bitcast.116), channel_id=1, source_target_pairs={{0,1},{1,0},{2,3},{3,2},{4,5},{5,4},{6,7},{7,6},{8,9},{9,8},{10,11... | collective-permute-start | bytes 1474568 | tf_op jit(solution)/shard_map/ppermute | solution.py:723
  46.6 14.9 %collective-permute-start.12 = (bf16[8,48,640]{2,1,0:T(8,128)(2,1)S(1)}, bf16[8,48,640]{2,1,0:T(8,128)(2,1)S(1)}, u32[]{:S(2)}, u32[]{:S(2)}) collective-permute-start(bf16[8,48,640]{2,1,0:T(8,128)(2,1)S(1)} %bitcast.118), channel_id=1, source_target_pairs={{0,1},{1,0},{2,3},{3,2},{4,5},{5,4},{6,7},{7,6},{8,9},{9,8},{10,11... | collective-permute-start | bytes 1474568 | tf_op jit(solution)/shard_map/ppermute | solution.py:723
  47.1 14.4 %collective-permute-start.15 = (bf16[8,48,640]{2,1,0:T(8,128)(2,1)S(1)}, bf16[8,48,640]{2,1,0:T(8,128)(2,1)S(1)}, u32[]{:S(2)}, u32[]{:S(2)}) collective-permute-start(bf16[8,48,640]{2,1,0:T(8,128)(2,1)S(1)} %bitcast.137), channel_id=1, source_target_pairs={{0,1},{1,0},{2,3},{3,2},{4,5},{5,4},{6,7},{7,6},{8,9},{9,8},{10,11... | collective-permute-start | bytes 1474568 | tf_op jit(solution)/shard_map/ppermute | solution.py:723
  54.8 8.3 %collective-permute-start.13 = (bf16[8,48,640]{2,1,0:T(8,128)(2,1)S(1)}, bf16[8,48,640]{2,1,0:T(8,128)(2,1)}, u32[]{:S(2)}, u32[]{:S(2)}) collective-permute-start(bf16[8,48,640]{2,1,0:T(8,128)(2,1)S(1)} %bitcast.139), channel_id=1, source_target_pairs={{0,1},{1,0},{2,3},{3,2},{4,5},{5,4},{6,7},{7,6},{8,9},{9,8},{10,11... | collective-permute-start | bytes 1474568 | tf_op jit(solution)/shard_map/ppermute | solution.py:723
  60.3 14.6 %collective-permute-start.16 = (bf16[2,2,48,1664]{3,2,1,0:T(8,128)(2,1)S(1)}, bf16[2,2,48,1664]{3,2,1,0:T(8,128)(2,1)}, u32[]{:S(2)}, u32[]{:S(2)}) collective-permute-start(bf16[2,2,48,1664]{3,2,1,0:T(8,128)(2,1)S(1)} %get-tuple-element.225), channel_id=1, source_target_pairs={{0,16},{1,17},{2,18},{3,19},{4,20},{5,21},{6,22},{7,23},{8,24},{9,... | collective-permute-start | bytes 1916936 | tf_op jit(solution)/shard_map/ppermute | solution.py:723
  60.9 15.8 %collective-permute-start.8 = (bf16[2,2,48,1792]{3,2,1,0:T(8,128)(2,1)S(1)}, bf16[2,2,48,1792]{3,2,1,0:T(8,128)(2,1)S(1)}, u32[]{:S(2)}, u32[]{:S(2)}) collective-permute-start(bf16[2,2,48,1792]{3,2,1,0:T(8,128)(2,1)S(1)} %get-tuple-element.223), channel_id=1, source_target_pairs={{0,8},{1,9},{2,10},{3,11},{4,12},{5,13},{6,14},{7,15},{8,0},{9,1},... | collective-permute-start | bytes 2064392 | tf_op jit(solution)/shard_map/ppermute | solution.py:723
  76.1 17.5 %copy-start.23 = (bf16[2,2,2,48,1664]{4,3,2,1,0:T(8,128)(2,1)}, bf16[2,2,2,48,1664]{4,3,2,1,0:T(8,128)(2,1)S(1)}, u32[]{:S(2)}) copy-start(bf16[2,2,2,48,1664]{4,3,2,1,0:T(8,128)(2,1)S(1)} %pad_maximum_fusion.1) | copy-start | bytes 3833860
  76.1 33.5 %collective-permute-start.20 = (bf16[2,2,2,48,1664]{4,3,2,1,0:T(8,128)(2,1)S(1)}, bf16[2,2,2,48,1664]{4,3,2,1,0:T(8,128)(2,1)}, u32[]{:S(2)}, u32[]{:S(2)}) collective-permute-start(bf16[2,2,2,48,1664]{4,3,2,1,0:T(8,128)(2,1)S(1)} %pad_maximum_fusion.1), channel_id=1, source_target_pairs={{0,8},{1,9},{2,10},{3,11},{4,12},{5,13},{6,14},{7,15},{8,0},{9,1},... | collective-permute-start | bytes 3833864 | tf_op jit(solution)/shard_map/ppermute | solution.py:723
  76.7 16.9 %collective-permute-start.19 = (bf16[8,48,1664]{2,1,0:T(8,128)(2,1)S(1)}, bf16[8,48,1664]{2,1,0:T(8,128)(2,1)}, u32[]{:S(2)}, u32[]{:S(2)}) collective-permute-start(bf16[8,48,1664]{2,1,0:T(8,128)(2,1)S(1)} %bitcast.110), channel_id=1, source_target_pairs={{0,1},{1,0},{2,3},{3,2},{4,5},{5,4},{6,7},{7,6},{8,9},{9,8},{10,11... | collective-permute-start | bytes 3833864 | tf_op jit(solution)/shard_map/ppermute | solution.py:723
  76.8 32.8 %collective-permute-start.17 = (bf16[2,2,2,48,1792]{4,3,2,1,0:T(8,128)(2,1)S(1)}, bf16[2,2,2,48,1792]{4,3,2,1,0:T(8,128)(2,1)}, u32[]{:S(2)}, u32[]{:S(2)}) collective-permute-start(bf16[2,2,2,48,1792]{4,3,2,1,0:T(8,128)(2,1)S(1)} %pad_maximum_fusion), channel_id=1, source_target_pairs={{0,16},{1,17},{2,18},{3,19},{4,20},{5,21},{6,22},{7,23},{8,24},{9,... | collective-permute-start | bytes 4128776 | tf_op jit(solution)/shard_map/ppermute | solution.py:723
  79.1 14.5 %collective-permute-start.18 = (bf16[8,48,1792]{2,1,0:T(8,128)(2,1)S(1)}, bf16[8,48,1792]{2,1,0:T(8,128)(2,1)}, u32[]{:S(2)}, u32[]{:S(2)}) collective-permute-start(bf16[8,48,1792]{2,1,0:T(8,128)(2,1)S(1)} %bitcast.108), channel_id=1, source_target_pairs={{0,1},{1,0},{2,3},{3,2},{4,5},{5,4},{6,7},{7,6},{8,9},{9,8},{10,11... | collective-permute-start | bytes 4128776 | tf_op jit(solution)/shard_map/ppermute | solution.py:723
  109.6 5.2 %collective-permute-start.21 = (bf16[8,48,1792]{2,1,0:T(8,128)(2,1)}, bf16[8,48,1792]{2,1,0:T(8,128)(2,1)S(1)}, u32[]{:S(2)}, u32[]{:S(2)}) collective-permute-start(bf16[8,48,1792]{2,1,0:T(8,128)(2,1)} %bitcast.41.rest_1_), channel_id=1, source_target_pairs={{0,1},{1,0},{2,3},{3,2},{4,5},{5,4},{6,7},{7,6},{8,9},{9,8},{10,11... | collective-permute-start | bytes 4128776 | tf_op jit(solution)/shard_map/ppermute | solution.py:723
  109.6 5.2 %collective-permute-start.22 = (bf16[8,48,1664]{2,1,0:T(8,128)(2,1)}, bf16[8,48,1664]{2,1,0:T(8,128)(2,1)S(1)}, u32[]{:S(2)}, u32[]{:S(2)}) collective-permute-start(bf16[8,48,1664]{2,1,0:T(8,128)(2,1)} %bitcast.42.rest_3_), channel_id=1, source_target_pairs={{0,1},{1,0},{2,3},{3,2},{4,5},{5,4},{6,7},{7,6},{8,9},{9,8},{10,11... | collective-permute-start | bytes 3833864 | tf_op jit(solution)/shard_map/ppermute | solution.py:723
  162.5 9.8 %collective-permute-start.23 = (bf16[16,24,3072]{2,1,0:T(8,128)(2,1)}, bf16[16,24,3072]{2,1,0:T(8,128)(2,1)S(1)}, u32[]{:S(2)}, u32[]{:S(2)}) collective-permute-start(bf16[16,24,3072]{2,1,0:T(8,128)(2,1)} %get-tuple-element.149), channel_id=1, source_target_pairs={{0,1},{1,0},{2,3},{3,2},{4,5},{5,4},{6,7},{7,6},{8,9},{9,8},{10,11... | collective-permute-start | bytes 7077896 | tf_op jit(solution)/shard_map/ppermute | solution.py:723
  171.9 4.8 %collective-permute-start.24 = (bf16[16,24,3072]{2,1,0:T(8,128)(2,1)}, bf16[16,24,3072]{2,1,0:T(8,128)(2,1)S(1)}, u32[]{:S(2)}, u32[]{:S(2)}) collective-permute-start(bf16[16,24,3072]{2,1,0:T(8,128)(2,1)} %get-tuple-element.152), channel_id=1, source_target_pairs={{0,1},{1,0},{2,3},{3,2},{4,5},{5,4},{6,7},{7,6},{8,9},{9,8},{10,11... | collective-permute-start | bytes 7077896 | tf_op jit(solution)/shard_map/ppermute | solution.py:723
  178.3 28.3 %collective-permute-start.26 = (bf16[2,4,24,3072]{3,2,1,0:T(8,128)(2,1)S(1)}, bf16[2,4,24,3072]{3,2,1,0:T(8,128)(2,1)S(1)}, u32[]{:S(2)}, u32[]{:S(2)}) collective-permute-start(bf16[2,4,24,3072]{3,2,1,0:T(8,128)(2,1)S(1)} %get-tuple-element.169), channel_id=1, source_target_pairs={{0,16},{1,17},{2,18},{3,19},{4,20},{5,21},{6,22},{7,23},{8,24},{9,... | collective-permute-start | bytes 3538952 | tf_op jit(solution)/shard_map/ppermute | solution.py:723
  179.4 28.0 %collective-permute-start.25 = (bf16[2,4,24,3072]{3,2,1,0:T(8,128)(2,1)S(1)}, bf16[2,4,24,3072]{3,2,1,0:T(8,128)(2,1)S(1)}, u32[]{:S(2)}, u32[]{:S(2)}) collective-permute-start(bf16[2,4,24,3072]{3,2,1,0:T(8,128)(2,1)S(1)} %get-tuple-element.168), channel_id=1, source_target_pairs={{0,8},{1,9},{2,10},{3,11},{4,12},{5,13},{6,14},{7,15},{8,0},{9,1},... | collective-permute-start | bytes 3538952 | tf_op jit(solution)/shard_map/ppermute | solution.py:723
  208.8 14.5 %collective-permute-start.27 = (bf16[4,24,3072]{2,1,0:T(8,128)(2,1)S(1)}, bf16[4,24,3072]{2,1,0:T(8,128)(2,1)S(1)}, u32[]{:S(2)}, u32[]{:S(2)}) collective-permute-start(bf16[4,24,3072]{2,1,0:T(8,128)(2,1)S(1)} %get-tuple-element.176), channel_id=1, source_target_pairs={{0,16},{1,17},{2,18},{3,19},{4,20},{5,21},{6,22},{7,23},{8,24},{9,... | collective-permute-start | bytes 1769480 | tf_op jit(solution)/shard_map/ppermute | solution.py:723
  209.9 14.2 %collective-permute-start.28 = (bf16[4,24,3072]{2,1,0:T(8,128)(2,1)S(1)}, bf16[4,24,3072]{2,1,0:T(8,128)(2,1)S(1)}, u32[]{:S(2)}, u32[]{:S(2)}) collective-permute-start(bf16[4,24,3072]{2,1,0:T(8,128)(2,1)S(1)} %get-tuple-element.178), channel_id=1, source_target_pairs={{0,8},{1,9},{2,10},{3,11},{4,12},{5,13},{6,14},{7,15},{8,0},{9,1},... | collective-permute-start | bytes 1769480 | tf_op jit(solution)/shard_map/ppermute | solution.py:723
  218.2 10.6 %collective-permute-start.29 = (bf16[16,24,1536]{2,1,0:T(8,128)(2,1)S(1)}, bf16[16,24,1536]{2,1,0:T(8,128)(2,1)S(1)}, u32[]{:S(2)}, u32[]{:S(2)}) collective-permute-start(bf16[16,24,1536]{2,1,0:T(8,128)(2,1)S(1)} %get-tuple-element.181), channel_id=1, source_target_pairs={{0,1},{1,0},{2,3},{3,2},{4,5},{5,4},{6,7},{7,6},{8,9},{9,8},{10,11... | collective-permute-start | bytes 3538952 | tf_op jit(solution)/shard_map/ppermute | solution.py:723
  218.3 10.6 %collective-permute-start.30 = (bf16[16,24,1536]{2,1,0:T(8,128)(2,1)S(1)}, bf16[16,24,1536]{2,1,0:T(8,128)(2,1)S(1)}, u32[]{:S(2)}, u32[]{:S(2)}) collective-permute-start(bf16[16,24,1536]{2,1,0:T(8,128)(2,1)S(1)} %get-tuple-element.183), channel_id=1, source_target_pairs={{0,1},{1,0},{2,3},{3,2},{4,5},{5,4},{6,7},{7,6},{8,9},{9,8},{10,11... | collective-permute-start | bytes 3538952 | tf_op jit(solution)/shard_map/ppermute | solution.py:723
  224.9 17.7 %collective-permute-start.32 = (bf16[2,24,6144]{2,1,0:T(8,128)(2,1)S(1)}, bf16[2,24,6144]{2,1,0:T(8,128)(2,1)S(1)}, u32[]{:S(2)}, u32[]{:S(2)}) collective-permute-start(bf16[2,24,6144]{2,1,0:T(8,128)(2,1)S(1)} %get-tuple-element.194), channel_id=1, source_target_pairs={{0,2},{1,3},{2,0},{3,1},{4,6},{5,7},{6,4},{7,5},{8,10},{9,11},{10,... | collective-permute-start | bytes 1769480 | tf_op jit(solution)/shard_map/ppermute | solution.py:723
  230.6 13.1 %collective-permute-start.33 = (bf16[2,4,24,1536]{3,2,1,0:T(8,128)(2,1)S(1)}, bf16[2,4,24,1536]{3,2,1,0:T(8,128)(2,1)S(1)}, u32[]{:S(2)}, u32[]{:S(2)}) collective-permute-start(bf16[2,4,24,1536]{3,2,1,0:T(8,128)(2,1)S(1)} %get-tuple-element.197), channel_id=1, source_target_pairs={{0,8},{1,9},{2,10},{3,11},{4,12},{5,13},{6,14},{7,15},{8,0},{9,1},... | collective-permute-start | bytes 1769480 | tf_op jit(solution)/shard_map/ppermute | solution.py:723
  231.2 12.9 %collective-permute-start.34 = (bf16[2,4,24,1536]{3,2,1,0:T(8,128)(2,1)S(1)}, bf16[2,4,24,1536]{3,2,1,0:T(8,128)(2,1)S(1)}, u32[]{:S(2)}, u32[]{:S(2)}) collective-permute-start(bf16[2,4,24,1536]{3,2,1,0:T(8,128)(2,1)S(1)} %get-tuple-element.199), channel_id=1, source_target_pairs={{0,16},{1,17},{2,18},{3,19},{4,20},{5,21},{6,22},{7,23},{8,24},{9,... | collective-permute-start | bytes 1769480 | tf_op jit(solution)/shard_map/ppermute | solution.py:723
  245.2 9.0 %collective-permute-start.38 = (bf16[4,24,1536]{2,1,0:T(8,128)(2,1)S(1)}, bf16[4,24,1536]{2,1,0:T(8,128)(2,1)S(1)}, u32[]{:S(2)}, u32[]{:S(2)}) collective-permute-start(bf16[4,24,1536]{2,1,0:T(8,128)(2,1)S(1)} %get-tuple-element.202), channel_id=1, source_target_pairs={{0,16},{1,17},{2,18},{3,19},{4,20},{5,21},{6,22},{7,23},{8,24},{9,... | collective-permute-start | bytes 884744 | tf_op jit(solution)/shard_map/ppermute | solution.py:723
  245.9 9.6 %collective-permute-start.39 = (bf16[4,24,1536]{2,1,0:T(8,128)(2,1)S(1)}, bf16[4,24,1536]{2,1,0:T(8,128)(2,1)S(1)}, u32[]{:S(2)}, u32[]{:S(2)}) collective-permute-start(bf16[4,24,1536]{2,1,0:T(8,128)(2,1)S(1)} %get-tuple-element.203), channel_id=1, source_target_pairs={{0,8},{1,9},{2,10},{3,11},{4,12},{5,13},{6,14},{7,15},{8,0},{9,1},... | collective-permute-start | bytes 884744 | tf_op jit(solution)/shard_map/ppermute | solution.py:723
  247.5 12.7 %collective-permute-start.40 = (bf16[24,6144]{1,0:T(8,128)(2,1)S(1)}, bf16[24,6144]{1,0:T(8,128)(2,1)S(1)}, u32[]{:S(2)}, u32[]{:S(2)}) collective-permute-start(bf16[24,6144]{1,0:T(8,128)(2,1)S(1)} %get-tuple-element.205), channel_id=1, source_target_pairs={{0,4},{1,5},{2,6},{3,7},{4,0},{5,1},{6,2},{7,3},{8,12},{9,13},{10,... | collective-permute-start | bytes 884744 | tf_op jit(solution)/shard_map/ppermute | solution.py:723
  250.7 1.2 collective-permute-start.31
  251.9 9.2 %collective-permute-start.35 = (f32[1,9984]{1,0:T(1,128)S(1)}, f32[1,9984]{1,0:T(1,128)S(1)}, u32[]{:S(2)}, u32[]{:S(2)}) collective-permute-start(f32[1,9984]{1,0:T(1,128)S(1)} %add.63), channel_id=1, source_target_pairs={{0,8},{1,9},{2,10},{3,11},{4,12},{5,13},{6,14},{7,15},{8,0},{9,1},... | collective-permute-start | bytes 119816 | tf_op jit(solution)/shard_map/ppermute | solution.py:723
  253.1 8.0 %collective-permute-start.36 = (f32[1,9984]{1,0:T(1,128)S(1)}, f32[1,9984]{1,0:T(1,128)S(1)}, u32[]{:S(2)}, u32[]{:S(2)}) collective-permute-start(f32[1,9984]{1,0:T(1,128)S(1)} %add.63), channel_id=1, source_target_pairs={{0,16},{1,17},{2,18},{3,19},{4,20},{5,21},{6,22},{7,23},{8,24},{9,... | collective-permute-start | bytes 119816 | tf_op jit(solution)/shard_map/ppermute | solution.py:723
  254.2 6.9 %collective-permute-start.37 = (f32[1,9984]{1,0:T(1,128)S(1)}, f32[1,9984]{1,0:T(1,128)S(1)}, u32[]{:S(2)}, u32[]{:S(2)}) collective-permute-start(f32[1,9984]{1,0:T(1,128)S(1)} %add.63), channel_id=1, source_target_pairs={{0,24},{1,25},{2,26},{3,27},{4,28},{5,29},{6,30},{7,31},{8,16},{9,... | collective-permute-start | bytes 119816 | tf_op jit(solution)/shard_map/ppermute | solution.py:723
  261.9 9.5 %collective-permute-start.44 = (bf16[2,24,3072]{2,1,0:T(8,128)(2,1)S(1)}, bf16[2,24,3072]{2,1,0:T(8,128)(2,1)S(1)}, u32[]{:S(2)}, u32[]{:S(2)}) collective-permute-start(bf16[2,24,3072]{2,1,0:T(8,128)(2,1)S(1)} %get-tuple-element.213), channel_id=1, source_target_pairs={{0,2},{1,3},{2,0},{3,1},{4,6},{5,7},{6,4},{7,5},{8,10},{9,11},{10,... | collective-permute-start | bytes 884744 | tf_op jit(solution)/shard_map/ppermute | solution.py:723
  262.0 10.9 %collective-permute-start.41 = (f32[1,9984]{1,0:T(1,128)S(1)}, f32[1,9984]{1,0:T(1,128)S(1)}, u32[]{:S(2)}, u32[]{:S(2)}) collective-permute-start(f32[1,9984]{1,0:T(1,128)S(1)} %add_add_fusion.1), channel_id=1, source_target_pairs={{0,2},{1,3},{2,0},{3,1},{4,6},{5,7},{6,4},{7,5},{8,10},{9,11},{10,... | collective-permute-start | bytes 119816 | tf_op jit(solution)/shard_map/ppermute | solution.py:723
  264.0 8.9 %collective-permute-start.42 = (f32[1,9984]{1,0:T(1,128)S(1)}, f32[1,9984]{1,0:T(1,128)S(1)}, u32[]{:S(2)}, u32[]{:S(2)}) collective-permute-start(f32[1,9984]{1,0:T(1,128)S(1)} %add_add_fusion.1), channel_id=1, source_target_pairs={{0,4},{1,5},{2,6},{3,7},{4,0},{5,1},{6,2},{7,3},{8,12},{9,13},{10,... | collective-permute-start | bytes 119816 | tf_op jit(solution)/shard_map/ppermute | solution.py:723
  265.2 8.9 %collective-permute-start.43 = (f32[1,9984]{1,0:T(1,128)S(1)}, f32[1,9984]{1,0:T(1,128)S(1)}, u32[]{:S(2)}, u32[]{:S(2)}) collective-permute-start(f32[1,9984]{1,0:T(1,128)S(1)} %add_add_fusion.1), channel_id=1, source_target_pairs={{0,6},{1,7},{2,4},{3,5},{4,2},{5,3},{6,0},{7,1},{8,14},{9,15},{10,... | collective-permute-start | bytes 119816 | tf_op jit(solution)/shard_map/ppermute | solution.py:723
  272.0 7.2 %collective-permute-start.45 = (bf16[24,3072]{1,0:T(8,128)(2,1)S(1)}, bf16[24,3072]{1,0:T(8,128)(2,1)S(1)}, u32[]{:S(2)}, u32[]{:S(2)}) collective-permute-start(bf16[24,3072]{1,0:T(8,128)(2,1)S(1)} %get-tuple-element.218), channel_id=1, source_target_pairs={{0,4},{1,5},{2,6},{3,7},{4,0},{5,1},{6,2},{7,3},{8,12},{9,13},{10,... | collective-permute-start | bytes 442376 | tf_op jit(solution)/shard_map/ppermute | solution.py:723
  (31 other events, 154.0 us)
